TPU v7x, 32 devices: a whole 2x2x4 slice. The times are simulated.
32 devices in a mesh: dp: 8 (over z, x), tensor: 4 (over y, core).
Axes of the slice: x: 2, y: 2, z: 4, core: 2. Of those that a mesh axis runs over, the one named last changes fastest.
Arguments:
- tokens: bfloat16 [16384, 1024], P(('dp', 'tensor')), may hold values from -6 to 6
- out_grad: bfloat16 [16384, 1024], P(('dp', 'tensor')), may hold values from -6 to 6
- seq_lengths: int32 [16], P('dp'), may hold values from 256 to 1024, as said below
- norm_gains: float32 [2, 1024], replicated, may hold values from 0.25 to 1.75
- row_biases: float32 [4, 1024], replicated, may hold values from -1.5 to 1.5
- qkv_weight: bfloat16 [1024, 3072], P('dp', 'tensor'), may hold values from -0.1875 to 0.1875
- qkv_bias: float32 [3072], P('tensor'), may hold values from -2.5 to 2.5
- dense_weight: bfloat16 [1024, 1024], P('tensor', 'dp'), may hold values from -0.75 to 0.75
- fc1_weight: bfloat16 [1024, 4096], P('dp', 'tensor'), may hold values from -0.1875 to 0.1875
- fc1_bias: float32 [4096], P('tensor'), may hold values from -2.5 to 2.5
- fc2_weight: bfloat16 [4096, 1024], P('tensor', 'dp'), may hold values from -0.09375 to 0.09375
- block_slot: int32 [768], replicated, may hold values from 0 to 767, as said below
- left_stat: float32 [768, 128, 128], P(('dp', 'tensor'))
- right_stat: float32 [768, 128, 128], P(('dp', 'tensor'))
- left_root: float32 [768, 128, 128], P(('dp', 'tensor'))
- right_root: float32 [768, 128, 128], P(('dp', 'tensor'))
- row_accum: float32 [6, 1024], replicated, may hold values from 0.5 to 2
- qkv_bias_accum: float32 [3072], P('tensor'), may hold values from 0.5 to 2
- fc1_bias_accum: float32 [4096], P('tensor'), may hold values from 0.5 to 2
Outputs:
- layer_out: bfloat16 [16384, 1024], P(('dp', 'tensor'))
- input_grad: float32 [16384, 1024], P(('dp', 'tensor'))
- block_grad: float32 [768, 128, 128], P(('dp', 'tensor'))
- left_new: float32 [768, 128, 128], P(('dp', 'tensor'))
- right_new: float32 [768, 128, 128], P(('dp', 'tensor'))
- block_update: float32 [768, 128, 128], P(('dp', 'tensor'))
- row_accum_new: float32 [6, 1024], replicated
- row_update: float32 [6, 1024], replicated
- qkv_bias_accum_new: float32 [3072], P('tensor')
- qkv_bias_update: float32 [3072], P('tensor')
- fc1_bias_accum_new: float32 [4096], P('tensor')
- fc1_bias_update: float32 [4096], P('tensor')
Inputs may be any that keep to these rules, and one draw needn't show every extreme that they name: `seq_lengths`: some sequence has exactly 1024 real tokens. `block_slot`: a permutation of the 768 slots; block t * 192 + j gets a slot s for which (s // 24) modulo the tensor axis's size is t.
All inputs are finite; a program needn't handle non-finite values.
Results may differ from a plain program's by a relative error of at most 0.0088.
Values may be sent and summed in bfloat16 or wider, within the bound.
A program may use at most 192 MiB of HBM per device.

v0:
```python
import math

import jax
import jax.numpy as jnp
from jax import lax
from jax.sharding import PartitionSpec as P

HEAD = 64
ROT = 16
LEN = 1024
BLOCK = 128


highest = lax.Precision.HIGHEST
masked_score = -1e30
shampoo_rate = 0.03
adagrad_rate = 0.1
stat_decay = 0.5


def layer_norm(values, gain_vec, shift_vec):
    average = jnp.mean(values, axis=-1, keepdims=True)
    centered = values - average
    variance = jnp.mean(centered * centered, axis=-1, keepdims=True)
    return centered * lax.rsqrt(variance + 1e-05) * gain_vec + shift_vec


def both_norms(values, gain_pair, shift_pair):
    return (
        layer_norm(values, gain_pair[0], shift_pair[0]),
        layer_norm(values, gain_pair[1], shift_pair[1]),
    )


def gelu_exact(values):
    return jax.nn.gelu(values, approximate=False)


def rotary_tables():
    half_rot = ROT // 2
    exponent = jnp.arange(half_rot, dtype=jnp.float32) * (2.0 / ROT)
    inverse = jnp.power(10000.0, -exponent)
    angles = jnp.arange(LEN, dtype=jnp.float32)[:, None] * inverse[None, :]
    return (jnp.cos(angles), jnp.sin(angles))


def apply_rotary(vectors, cosine, sine):
    half_rot = ROT // 2
    first_half = vectors[..., :half_rot]
    second = vectors[..., half_rot:ROT]
    cos_wide = cosine[:, None, :]
    sin_wide = sine[:, None, :]
    rot_first = first_half * cos_wide - second * sin_wide
    rot_second = second * cos_wide + first_half * sin_wide
    return jnp.concatenate([rot_first, rot_second, vectors[..., ROT:]], axis=-1)


def rotary_back(grads, cosine, sine):
    half_rot = ROT // 2
    first_half = grads[..., :half_rot]
    second = grads[..., half_rot:ROT]
    cos_wide = cosine[:, None, :]
    sin_wide = sine[:, None, :]
    back_first = first_half * cos_wide + second * sin_wide
    back_second = second * cos_wide - first_half * sin_wide
    return jnp.concatenate([back_first, back_second, grads[..., ROT:]], axis=-1)


def visible(block_start, block_rows, limit):
    query_pos = block_start + jnp.arange(block_rows)
    key_pos = jnp.arange(LEN)
    return (key_pos[None, :] <= query_pos[:, None]) & (key_pos[None, :] < limit)


def block_scores(query_block, keys_seq, limit, block_start):
    block_rows = query_block.shape[0]
    scores = jnp.einsum(
        "qhd,khd->hqk", query_block, keys_seq, preferred_element_type=jnp.float32
    ) * (1.0 / math.sqrt(HEAD))
    return jnp.where(visible(block_start, block_rows, limit)[None], scores, masked_score)


def cut_blocks(matrix):
    rows_all, cols_all = matrix.shape
    shaped = matrix.reshape(rows_all // BLOCK, BLOCK, cols_all // BLOCK, BLOCK)
    return shaped.transpose(0, 2, 1, 3).reshape(-1, BLOCK, BLOCK)


def adagrad_step(grad_vec, accum):
    accum_next = accum + grad_vec * grad_vec
    return (accum_next, -adagrad_rate * grad_vec * lax.rsqrt(accum_next))


def shards(
    tokens,
    out_grad,
    seq_lengths,
    norm_gains,
    row_biases,
    qkv_weight,
    qkv_bias,
    dense_weight,
    fc1_weight,
    fc1_bias,
    fc2_weight,
    block_slot,
    left_stat,
    right_stat,
    left_root,
    right_root,
    row_accum,
    qkv_bias_accum,
    fc1_bias_accum,
):
    tensor_count = lax.axis_size("tensor")
    dp_count = lax.axis_size("dp")
    tensor_rank = lax.axis_index("tensor")
    own_rows = tokens.shape[0]
    group_rows = own_rows * tensor_count
    group_seqs = seq_lengths.shape[0]
    total_tokens = group_rows * dp_count
    grad_scale = 1.0 / math.sqrt(total_tokens)
    block_rows = min(512, LEN)
    block_count = LEN // block_rows
    row_ids = tensor_rank * own_rows + jnp.arange(own_rows)
    seq_ids = row_ids // LEN
    positions = row_ids % LEN
    seq_match = seq_ids[:, None] == jnp.arange(group_seqs)[None, :]
    row_limit = jnp.sum(jnp.where(seq_match, seq_lengths[None, :], 0), axis=1)
    row_valid = (positions < row_limit).astype(jnp.float32)
    inputs = tokens.astype(jnp.float32)
    (normed_attn, normed_mlp), norm_pullback = jax.vjp(
        both_norms, inputs, norm_gains, row_biases[:2]
    )
    all_attn, all_mlp = (
        lax.all_gather(normed_attn.astype(jnp.bfloat16), "tensor", axis=0, tiled=True),
        lax.all_gather(normed_mlp.astype(jnp.bfloat16), "tensor", axis=0, tiled=True),
    )
    full_qkv, full_dense, full_fc1, full_fc2 = (
        lax.all_gather(qkv_weight, "dp", axis=0, tiled=True),
        lax.all_gather(dense_weight, "dp", axis=1, tiled=True),
        lax.all_gather(fc1_weight, "dp", axis=0, tiled=True),
        lax.all_gather(fc2_weight, "dp", axis=1, tiled=True),
    )
    projected = jnp.dot(all_attn, full_qkv, preferred_element_type=jnp.float32) + qkv_bias
    heads_local = projected.shape[1] // (3 * HEAD)
    shaped = projected.reshape(group_seqs, LEN, heads_local, 3 * HEAD)
    cosine, sine = rotary_tables()
    queries = apply_rotary(shaped[..., :HEAD], cosine, sine).astype(jnp.bfloat16)
    keys_all = apply_rotary(shaped[..., HEAD : 2 * HEAD], cosine, sine).astype(jnp.bfloat16)
    values = shaped[..., 2 * HEAD :].astype(jnp.bfloat16)

    def forward_seq(seq_items):
        queries_seq, keys_seq, values_seq, limit = seq_items

        def one_block(block_index):
            block_start = block_index * block_rows
            query_block = lax.dynamic_slice_in_dim(queries_seq, block_start, block_rows, 0)
            scores = block_scores(query_block, keys_seq, limit, block_start)
            row_max = jnp.max(scores, axis=-1, keepdims=True)
            unnormed = jnp.exp(scores - row_max)
            row_total = jnp.sum(unnormed, axis=-1, keepdims=True)
            probabilities = (unnormed / row_total).astype(jnp.bfloat16)
            context = jnp.einsum(
                "hqk,khd->qhd", probabilities, values_seq, preferred_element_type=jnp.float32
            )
            return (context, (row_max + jnp.log(row_total))[..., 0])

        context_blocks, lse_blocks = lax.map(one_block, jnp.arange(block_count))
        return (context_blocks.reshape(LEN, heads_local, HEAD), lse_blocks)

    context_all, lse_all = lax.map(forward_seq, (queries, keys_all, values, seq_lengths))
    context_low = context_all.reshape(group_rows, heads_local * HEAD).astype(jnp.bfloat16)
    attn_part = jnp.dot(context_low, full_dense, preferred_element_type=jnp.float32)
    hidden_pre = jnp.dot(all_mlp, full_fc1, preferred_element_type=jnp.float32) + fc1_bias
    activated_full, gelu_pullback = jax.vjp(gelu_exact, hidden_pre)
    activated = activated_full.astype(jnp.bfloat16)
    mlp_part = jnp.dot(activated, full_fc2, preferred_element_type=jnp.float32)
    branch = lax.psum_scatter(attn_part + mlp_part, "tensor", scatter_dimension=0, tiled=True)
    layer_out = (inputs + branch + row_biases[2] + row_biases[3]).astype(jnp.bfloat16)
    back_qkv, back_dense, back_fc1, back_fc2 = (full_qkv, full_dense, full_fc1, full_fc2)
    grad_out = out_grad.astype(jnp.float32) * row_valid[:, None]
    all_grad = lax.all_gather(grad_out.astype(jnp.bfloat16), "tensor", axis=0, tiled=True)
    fc2_grad = jnp.einsum("rf,rd->fd", activated, all_grad, preferred_element_type=jnp.float32)
    act_grad = jnp.einsum("rd,fd->rf", all_grad, back_fc2, preferred_element_type=jnp.float32)
    pre_low = gelu_pullback(act_grad)[0].astype(jnp.bfloat16)
    fc1_bias_grad = jnp.sum(pre_low.astype(jnp.float32), axis=0)
    fc1_grad = jnp.einsum("rd,rf->df", all_mlp, pre_low, preferred_element_type=jnp.float32)
    mlp_norm_grad = jnp.einsum("rf,df->rd", pre_low, back_fc1, preferred_element_type=jnp.float32)
    dense_grad = jnp.einsum("rc,rd->cd", context_low, all_grad, preferred_element_type=jnp.float32)
    context_grad = jnp.einsum(
        "rd,cd->rc", all_grad, back_dense, preferred_element_type=jnp.float32
    ).astype(jnp.bfloat16)
    context_grad = context_grad.reshape(group_seqs, LEN, heads_local, HEAD)

    def backward_seq(seq_items):
        queries_seq, keys_seq, values_seq, limit, grad_seq, lse_seq = seq_items

        def back_block(carry, block_index):
            key_grad, value_grad = carry
            block_start = block_index * block_rows
            query_block = lax.dynamic_slice_in_dim(queries_seq, block_start, block_rows, 0)
            grad_block = lax.dynamic_slice_in_dim(grad_seq, block_start, block_rows, 0)
            scores = block_scores(query_block, keys_seq, limit, block_start)
            probabilities = jnp.exp(scores - lse_seq[block_index][..., None])
            value_grad = value_grad + jnp.einsum(
                "hqk,qhd->khd",
                probabilities.astype(jnp.bfloat16),
                grad_block,
                preferred_element_type=jnp.float32,
            )
            prob_grad = jnp.einsum(
                "qhd,khd->hqk", grad_block, values_seq, preferred_element_type=jnp.float32
            )
            row_delta = jnp.sum(probabilities * prob_grad, axis=-1, keepdims=True)
            score_grad = (probabilities * (prob_grad - row_delta)).astype(jnp.bfloat16)
            query_grad = jnp.einsum(
                "hqk,khd->qhd", score_grad, keys_seq, preferred_element_type=jnp.float32
            ) * (1.0 / math.sqrt(HEAD))
            key_grad = key_grad + jnp.einsum(
                "hqk,qhd->khd", score_grad, query_block, preferred_element_type=jnp.float32
            ) * (1.0 / math.sqrt(HEAD))
            return ((key_grad, value_grad), query_grad)

        zeros_seq = jnp.zeros(keys_seq.shape, jnp.float32)
        (key_grad, value_grad), query_blocks = lax.scan(
            back_block, (zeros_seq, zeros_seq), jnp.arange(block_count)
        )
        return (query_blocks.reshape(LEN, heads_local, HEAD), key_grad, value_grad)

    query_grads, key_grads, value_grads = lax.map(
        backward_seq, (queries, keys_all, values, seq_lengths, context_grad, lse_all)
    )
    proj_grad = jnp.concatenate(
        [rotary_back(query_grads, cosine, sine), rotary_back(key_grads, cosine, sine), value_grads],
        axis=-1,
    )
    proj_low = proj_grad.reshape(group_rows, heads_local * 3 * HEAD).astype(jnp.bfloat16)
    qkv_bias_grad = jnp.sum(proj_low.astype(jnp.float32), axis=0)
    qkv_grad = jnp.einsum("rd,re->de", all_attn, proj_low, preferred_element_type=jnp.float32)
    attn_norm_grad = jnp.einsum("re,de->rd", proj_low, back_qkv, preferred_element_type=jnp.float32)
    attn_own, mlp_own = (
        lax.psum_scatter(
            attn_norm_grad.astype(jnp.bfloat16), "tensor", scatter_dimension=0, tiled=True
        ).astype(jnp.float32),
        lax.psum_scatter(
            mlp_norm_grad.astype(jnp.bfloat16), "tensor", scatter_dimension=0, tiled=True
        ).astype(jnp.float32),
    )
    input_part, gain_grads, shift_grads = norm_pullback((attn_own, mlp_own))
    input_grad = grad_out + input_part
    out_bias_grad = jnp.sum(grad_out, axis=0)
    row_partial = jnp.concatenate([gain_grads, shift_grads, out_bias_grad[None]], axis=0)
    row_total = lax.psum(row_partial, ("dp", "tensor"))
    qkv_bias_total, fc1_bias_total = lax.psum((qkv_bias_grad, fc1_bias_grad), "dp")
    local_blocks = jnp.concatenate(
        [cut_blocks(qkv_grad), cut_blocks(dense_grad), cut_blocks(fc1_grad), cut_blocks(fc2_grad)],
        axis=0,
    )
    blocks_tensor = local_blocks.shape[0]
    per_dev = blocks_tensor // dp_count
    my_slots = lax.dynamic_slice_in_dim(block_slot, tensor_rank * blocks_tensor, blocks_tensor)
    position = my_slots // per_dev // tensor_count * per_dev + my_slots % per_dev
    ordered = jnp.take(local_blocks, jnp.argsort(position), axis=0)
    own_grad = lax.psum_scatter(ordered, "dp", scatter_dimension=0, tiled=True) * grad_scale
    left_next = stat_decay * left_stat + (1.0 - stat_decay) * jnp.einsum(
        "sij,skj->sik", own_grad, own_grad, precision=highest
    )
    right_next = stat_decay * right_stat + (1.0 - stat_decay) * jnp.einsum(
        "sji,sjk->sik", own_grad, own_grad, precision=highest
    )
    pushed = jnp.einsum("sij,sjk->sik", left_root, own_grad, precision=highest)
    change = -shampoo_rate * jnp.einsum("sij,sjk->sik", pushed, right_root, precision=highest)
    row_grads = jnp.concatenate([row_total, row_total[4:5]], axis=0) * grad_scale
    row_next, row_change = adagrad_step(row_grads, row_accum)
    qkv_next, qkv_change = adagrad_step(qkv_bias_total * grad_scale, qkv_bias_accum)
    fc1_next, fc1_change = adagrad_step(fc1_bias_total * grad_scale, fc1_bias_accum)
    return (
        layer_out,
        input_grad,
        own_grad,
        left_next,
        right_next,
        change,
        row_next,
        row_change,
        qkv_next,
        qkv_change,
        fc1_next,
        fc1_change,
    )


def solution(mesh):
    return jax.shard_map(
        shards,
        mesh=mesh,
        in_specs=(
            P(("dp", "tensor"), None),
            P(("dp", "tensor"), None),
            P("dp"),
            P(),
            P(),
            P("dp", "tensor"),
            P("tensor"),
            P("tensor", "dp"),
            P("dp", "tensor"),
            P("tensor"),
            P("tensor", "dp"),
            P(),
            P(("dp", "tensor"), None, None),
            P(("dp", "tensor"), None, None),
            P(("dp", "tensor"), None, None),
            P(("dp", "tensor"), None, None),
            P(),
            P("tensor"),
            P("tensor"),
        ),
        out_specs=(
            P(("dp", "tensor"), None),
            P(("dp", "tensor"), None),
            P(("dp", "tensor"), None, None),
            P(("dp", "tensor"), None, None),
            P(("dp", "tensor"), None, None),
            P(("dp", "tensor"), None, None),
            P(),
            P(),
            P("tensor"),
            P("tensor"),
            P("tensor"),
            P("tensor"),
        ),
        check_vma=False,
    )
```

profile of v0, /device:TPU:0, one launch (start us, length us, event | category | flops | bytes accessed | tf_op | source)
XLA Modules:
  0.0 794.6 jit_solution(17565276090514532448)
XLA Ops:
  23.1 33.2 %all_gather.23 = bf16[256,1024]{1,0:T(8,128)(2,1)} all-gather(bf16[256,128]{1,0:T(8,128)(2,1)S(1)} %copy-done.32), channel_id=1, replica_groups=mesh['dp'=8,'tensor'=4] {'dp'}, dimensions={1}, use_global_device_ids=true | all-gather | bytes 589824 | tf_op jit(solution)/shard_map/all_gather | solution.py:141
  56.3 6.4 all-gather.9.cloned.1.call-done
  62.7 35.6 %all-gather.7.cloned.1.call-done = bf16[2048,1024]{1,0:T(8,128)(2,1)} async-done(((bf16[512,1024]{1,0:T(8,128)(2,1)}), bf16[2048,1024]{1,0:T(8,128)(2,1)}) %all-gather.7.cloned.1.call-update) | async-done | bytes 4194320 | tf_op jit(solution)/shard_map/all_gather | solution.py:136
  98.3 8.8 %convolution_add_fusion.1 = f32[2048,768]{1,0:T(8,128)} fusion(bf16[2048,1024]{1,0:T(8,128)(2,1)} %all-gather.7.cloned.1.call-done, bf16[1024,768]{1,0:T(8,128)(2,1)} %all-gather.9.cloned.1.call-done, f32[768]{0:T(1024)S(1)} %copy-done.50), kind=kOutput, calls=%fused_computation.87 | convolution fusion | flops 3222798336 | bytes 12061696 | tf_op jit(solution)/shard_map/dot_general | solution.py:145
  107.1 6.8 copy.79
  114.0 9.2 %reshape.320 = f32[2,1024,4,192]{1,0,3,2:T(2,128)} reshape(f32[2048,768]{0,1:T(8,128)} %copy.79) | data formatting | bytes 12582912 | tf_op jit(solution)/shard_map/reshape | solution.py:147
  123.1 4.9 convert.21
  137.7 51.9 %while.60 = (s32[]{:T(128)}, bf16[2,1024,4,64]{3,2,1,0:T(4,128)(2,1)}, f32[2,2,4,512]{3,2,1,0:T(4,128)S(1)}, bf16[2,1024,4,64]{1,3,2,0:T(8,128)(2,1)}, bf16[2,10...) while((s32[]{:T(128)}, ...), condition=%wide.region_7.8_spmd.clone, body=%wide.region_2.7_spmd.sunk.clone | while | flops 563084800 | bytes 34971060 | solution.py:172
  140.9 19.9 %while.59 = (s32[]{:T(128)}, bf16[2,512,4,64]{1,3,2,0:T(8,128)(2,1)}, f32[2,4,512]{2,1,0:T(4,128)S(1)}, s32[2]{0:T(128)S(1)}, s32[]{:T(128)}, /*index=5*/bf16[10...) while((s32[]{:T(128)}, ...), condition=%wide.region_6.6_spmd, body=%wide.region_3.5_spmd.sunk | while | flops 563084800 | bytes 29170368 | solution.py:169
  147.2 3.6 fusion.167
  157.2 3.6 fusion.167
  166.7 19.9 %while.59 = (s32[]{:T(128)}, bf16[2,512,4,64]{1,3,2,0:T(8,128)(2,1)}, f32[2,4,512]{2,1,0:T(4,128)S(1)}, s32[2]{0:T(128)S(1)}, s32[]{:T(128)}, /*index=5*/bf16[10...) while((s32[]{:T(128)}, ...), condition=%wide.region_6.6_spmd, body=%wide.region_3.5_spmd.sunk | while | flops 563084800 | bytes 29170368 | solution.py:169
  173.1 3.6 fusion.167
  183.0 3.6 fusion.167
  189.5 3.6 convolution_convert_fusion.2
  197.9 167.8 %while.62 = (s32[]{:T(128)}, f32[2,1024,4,64]{3,2,1,0:T(4,128)}, f32[2,1024,4,64]{1,3,2,0:T(8,128)}, bf16[2,1024,4,64]{1,3,2,0:T(8,128)(2,1)}, bf16[2,1024,4,64]...) while((s32[]{:T(128)}, f32[2,1024,4,64]{3,2,1,0:T(4,128)}, ...), condition=%wide.region_17.18_spmd.clone, body=%wide.region_13.17_spmd.sunk.clone | while | flops 1376124416 | bytes 147947344 | solution.py:231
  205.9 67.9 %while.61 = (s32[]{:T(128)}, f32[1024,4,64]{0,2,1:T(8,128)S(1)}, f32[1024,4,64]{0,2,1:T(8,128)}, f32[2,512,4,64]{1,3,2,0:T(8,128)}, s32[2]{0:T(128)S(1)}, /*inde...) while((s32[]{:T(128)}, f32[1024,4,64]{0,2,1:T(8,128)S(1)}, ...), condition=%wide.region_16.16_spmd.clone, body=%wide.region_14.15_spmd.clone.sunk | while | flops 1376124416 | bytes 124844480 | solution.py:226
  207.1 5.7 fusion.157
  215.9 6.9 multiply_reduce_fusion.2
  222.8 3.7 multiply_convert_fusion.3
  226.5 3.4 fusion.159
  233.8 5.8 fusion.160
  240.8 5.7 fusion.157
  249.6 7.1 multiply_reduce_fusion.2
  256.7 3.7 multiply_convert_fusion.3
  260.4 3.4 fusion.159
  267.7 6.1 fusion.160
  289.7 67.6 %while.61 = (s32[]{:T(128)}, f32[1024,4,64]{0,2,1:T(8,128)S(1)}, f32[1024,4,64]{0,2,1:T(8,128)}, f32[2,512,4,64]{1,3,2,0:T(8,128)}, s32[2]{0:T(128)S(1)}, /*inde...) while((s32[]{:T(128)}, f32[1024,4,64]{0,2,1:T(8,128)S(1)}, ...), condition=%wide.region_16.16_spmd.clone, body=%wide.region_14.15_spmd.clone.sunk | while | flops 1376124416 | bytes 124844480 | solution.py:226
  290.9 5.7 fusion.157
  299.7 6.9 multiply_reduce_fusion.2
  306.6 3.7 multiply_convert_fusion.3
  310.3 3.4 fusion.159
  317.6 5.8 fusion.160
  324.6 5.7 fusion.157
  333.3 6.9 multiply_reduce_fusion.2
  340.2 3.7 multiply_convert_fusion.3
  344.0 3.4 fusion.159
  351.2 6.1 fusion.160
  365.8 6.7 copy.91
  372.5 3.4 copy.93
  375.9 3.3 copy.94
  388.6 5.2 convolution_convert_fusion
  394.2 11.3 %fusion.84 = f32[2048,1024]{1,0:T(8,128)} fusion(bf16[2048,1024]{1,0:T(8,128)(2,1)} %all-gather.11.cloned.1.call-done, bf16[1024,1024]{1,0:T(8,128)(2,1)} %all-gather.13.cloned.1.call-done), kind=kOutput, calls=%fused_computation.201 | convolution fusion | flops 4294967296 | bytes 14680064 | tf_op jit(solution)/shard_map/dot_general | solution.py:175
  405.5 27.8 %convert_reduce_fusion = (f32[1024]{0:T(1024)S(1)}, bf16[2048,1024]{1,0:T(8,128)(2,1)S(1)}, f32[2048,1024]{1,0:T(8,128)}) fusion(f32[2048,1024]{1,0:T(8,128)} %fusion.84, f32[1024]{0:T(1024)S(1)} %copy-done.44, bf16[2048,1024]{1,0:T(8,128)(2,1)} %all-gather.17.cloned.1.call-done, bf16[1024,1024]{1,0:T(8,128)(2,1)} %all-gather.15.cloned.1.call-done), kind=kOutput, calls=%fused_computation.66 | convolution fusion | flops 4452252672 | bytes 27271168 | tf_op jit(solution)/shard_map/rd,fd->rf/dot_general | solution.py:185
  435.4 6.3 convolution_convert_fusion.1
  441.8 3.9 reshape.345
  445.7 12.2 %multiply_convert_fusion.1 = bf16[2048,1024]{1,0:T(8,128)(2,1)} fusion(f32[2048,1024]{1,0:T(8,128)} %get-tuple-element.383, f32[2048,1024]{1,0:T(8,128)} %fusion.84, f32[1024]{0:T(1024)S(1)} %copy-done.44), kind=kLoop, calls=%fused_computation.68 | loop fusion | flops 8388608 | bytes 20975616 | tf_op jit(solution)/shard_map/convert_element_type | solution.py:177
  457.9 6.3 fusion.85
  464.2 4.6 convolution_add_fusion
  474.3 6.5 copy.116
  480.8 6.5 copy.117
  487.4 7.8 convolution_bitcast_fusion
  501.5 4.6 convolution_bitcast_fusion.1
  512.8 3.4 fusion.86
  516.2 5.7 pad_maximum_fusion
  521.9 15.3 %gather_fusion = f32[192,128,128]{2,1,0:T(8,128)} fusion(f32[192,128,128]{2,1,0:T(8,128)} %pad_maximum_fusion, s32[1024]{0:T(1024)S(1)} %pad_clamp_fusion), kind=kCustom, calls=%fused_computation | custom fusion | bytes 25166592 | tf_op jit(solution)/shard_map/jit(_take)/gather | solution.py:264
  537.2 10.3 %broadcast_select_fusion = f32[192,128,128]{2,1,0:T(8,128)} fusion(f32[192,128,128]{2,1,0:T(8,128)} %gather_fusion, pred[192]{0:T(512)(128)(4,1)S(1)} %compare_and_fusion), kind=kLoop, calls=%fused_computation.83 | loop fusion | flops 3145728 | bytes 25166016 | tf_op jit(solution)/shard_map/jit(_take)/select_n | solution.py:264
  550.2 21.5 %all-reduce.4 = (f32[768]{0:T(1024)S(1)}, f32[1024]{0:T(1024)S(1)}) all-reduce(f32[768]{0:T(1024)S(1)} %reduce_sum.169, f32[1024]{0:T(1024)S(1)} %get-tuple-element.381), channel_id=1, replica_groups=mesh['dp'=8,'tensor'=4] {'dp'}, use_global_device_ids=true, to_apply=%region_30.31 | all-reduce | flops 1792 | bytes 14336 | tf_op jit(solution)/shard_map/psum | solution.py:255
  575.6 3.3 fusion.64
  579.0 4.7 fusion.66
  583.7 42.7 %psum.21 = f32[5,1024]{1,0:T(8,128)S(1)} all-reduce(f32[5,1024]{1,0:T(8,128)S(1)} %pad_maximum_fusion.3), channel_id=1, replica_groups=mesh['dp'=8,'tensor'=4] {'dp','tensor'}, use_global_device_ids=true, to_apply=%region_28.29 | all-reduce | flops 5120 | bytes 40960 | tf_op jit(solution)/shard_map/psum | solution.py:254
  627.1 145.8 %reduce-scatter.11.cloned.1.call-done = f32[24,128,128]{2,1,0:T(8,128)} async-done(((f32[192,128,128]{2,1,0:T(8,128)}), f32[24,128,128]{2,1,0:T(8,128)}) %reduce-scatter.11.cloned.1.call-update) | async-done | bytes 1572880 | tf_op jit(solution)/shard_map/reduce_scatter | solution.py:265
  776.1 3.9 add_multiply_fusion
  780.0 4.6 add_multiply_fusion.1
  (343 shorter events, 162.1 us)
Async XLA Ops:
  7.2 767.3 %copy-start = (f32[24,128,128]{2,1,0:T(8,128)S(1)}, f32[24,128,128]{2,1,0:T(8,128)}, u32[]{:S(2)}) copy-start(f32[24,128,128]{2,1,0:T(8,128)} %param.41) | copy-start | bytes 4718596
  7.2 10.1 %copy-start.45 = (s32[2]{0:T(128)S(1)}, s32[2]{0:T(128)}, u32[]{:S(2)}) copy-start(s32[2]{0:T(128)} %param.29) | copy-start | bytes 28
  7.2 10.7 %copy-start.13 = (bf16[512,1024]{1,0:T(8,128)(2,1)S(1)}, bf16[512,1024]{1,0:T(8,128)(2,1)}, u32[]{:S(2)}) copy-start(bf16[512,1024]{1,0:T(8,128)(2,1)} %param.28) | copy-start | bytes 3145732
  7.2 55.5 %all-gather.9.cloned.1.call-start = ((), (), s32[]{:S(2)}) async-start(), calls=%async_computation.5 | async-start | bytes 1769472 | tf_op jit(solution)/shard_map/all_gather | solution.py:140
  7.9 90.3 %all-gather.7.cloned.1.call-start = ((), (), s32[]{:S(2)}) async-start(), calls=%async_computation.4 | async-start | bytes 5242880 | tf_op jit(solution)/shard_map/all_gather | solution.py:136
  9.4 7.7 copy-start.30
  11.7 5.5 copy-start.34
  12.5 4.7 copy-start.28
  17.1 5.9 copy-start.32
  17.1 81.2 %copy-start.50 = (f32[768]{0:T(1024)S(1)}, f32[768]{0:T(1024)}, u32[]{:S(2)}) copy-start(f32[768]{0:T(1024)} %param.33) | copy-start | bytes 9220
  17.2 172.4 %all-gather.17.cloned.1.call-start = ((), (), s32[]{:S(2)}) async-start(), calls=%async_computation.10 | async-start | bytes 5242880 | tf_op jit(solution)/shard_map/all_gather | solution.py:183
  19.2 375.0 %all-gather.13.cloned.1.call-start = ((), (), s32[]{:S(2)}) async-start(), calls=%async_computation.7 | async-start | bytes 2359296 | tf_op jit(solution)/shard_map/all_gather | solution.py:142
  19.7 374.4 %all-gather.11.cloned.1.call-start = ((), (), s32[]{:S(2)}) async-start(), calls=%async_computation.6 | async-start | bytes 5242880 | tf_op jit(solution)/shard_map/all_gather | solution.py:137
  20.3 385.1 %all-gather.15.cloned.1.call-start = ((), (), s32[]{:S(2)}) async-start(), calls=%async_computation.8 | async-start | bytes 2359296 | tf_op jit(solution)/shard_map/all_gather | solution.py:143
  20.9 552.0 %reduce-scatter.9.cloned.1.call-start = ((), (), s32[]{:S(2)}) async-start(), calls=%async_computation.12 | async-start | bytes 5242880 | tf_op jit(solution)/shard_map/reduce_scatter | solution.py:243
  23.1 106.2 %copy-start.22 = (f32[1024,8]{0,1:T(8,128)}, f32[1024,8]{0,1:T(8,128)S(1)}, u32[]{:S(2)}) copy-start(f32[1024,8]{0,1:T(8,128)S(1)} %get-tuple-element.419) | copy-start | bytes 98308
  23.1 106.2 %copy-start.24 = (f32[1024,8]{0,1:T(8,128)}, f32[1024,8]{0,1:T(8,128)S(1)}, u32[]{:S(2)}) copy-start(f32[1024,8]{0,1:T(8,128)S(1)} %get-tuple-element.420) | copy-start | bytes 98308
  128.1 5.8 copy-start.10
  198.4 7.5 copy-start.8
  215.8 6.9 slice-start
  215.9 6.9 slice-start.1
  229.9 3.9 copy-start.2
  249.6 7.1 slice-start
  249.6 7.1 slice-start.1
  260.4 3.9 copy-start.5
  263.8 3.9 copy-start.2
  276.3 5.9 copy-start.9
  282.2 7.5 copy-start.8
  299.7 6.9 slice-start
  299.7 6.9 slice-start.1
  313.7 3.9 copy-start.2
  333.3 6.9 slice-start
  333.3 6.9 slice-start.1
  344.0 3.8 copy-start.5
  347.3 3.9 copy-start.2
  359.8 6.0 copy-start.9
  372.5 6.7 copy-start.23
  372.5 6.7 copy-start.25
  375.9 6.6 copy-start.20
  382.7 4.3 copy-start.7
  393.8 11.6 %copy-start.44 = (f32[1024]{0:T(1024)S(1)}, f32[1024]{0:T(1024)}, u32[]{:S(2)}) copy-start(f32[1024]{0:T(1024)} %param.36) | copy-start | bytes 12292
  393.9 179.1 %reduce-scatter.7.cloned.1.call-start = ((), (), s32[]{:S(2)}) async-start(), calls=%async_computation.11 | async-start | bytes 5242880 | tf_op jit(solution)/shard_map/reduce_scatter | solution.py:246
  405.5 29.9 %copy-start.47 = (bf16[1024,1024]{1,0:T(8,128)(2,1)S(1)}, bf16[1024,1024]{1,0:T(8,128)(2,1)}, u32[]{:S(2)}) copy-start(bf16[1024,1024]{1,0:T(8,128)(2,1)} %all-gather.13.cloned.1.call-done) | copy-start | bytes 6291460
  441.7 137.2 %reduce-scatter.5.cloned.1.call-start = ((), (), s32[]{:S(2)}) async-start(), calls=%async_computation.9 | async-start | bytes 10485760 | tf_op jit(solution)/shard_map/reduce_scatter | solution.py:179
  445.7 12.2 %copy-start.48 = (bf16[1024,1024]{1,0:T(8,128)(2,1)S(1)}, bf16[1024,1024]{1,0:T(8,128)(2,1)}, u32[]{:S(2)}) copy-start(bf16[1024,1024]{1,0:T(8,128)(2,1)} %all-gather.15.cloned.1.call-done) | copy-start | bytes 6291460
  457.9 6.4 copy-start.16
  468.8 304.1 %reduce-scatter.11.cloned.1.call-start = ((), (), s32[]{:S(2)}) async-start(), calls=%async_computation.13 | async-start | bytes 14155776 | tf_op jit(solution)/shard_map/reduce_scatter | solution.py:265
  496.1 5.4 copy-start.52
  547.5 24.2 %copy-start.42 = (f32[1024]{0:T(1024)S(1)}, f32[1024]{0:T(1024)}, u32[]{:S(2)}) copy-start(f32[1024]{0:T(1024)} %param.45) | copy-start | bytes 12292
  547.5 24.8 %copy-start.43 = (f32[768]{0:T(1024)S(1)}, f32[768]{0:T(1024)}, u32[]{:S(2)}) copy-start(f32[768]{0:T(1024)} %param.44) | copy-start | bytes 9220
  547.5 25.4 %copy-start.4 = (bf16[512,1024]{1,0:T(8,128)(2,1)S(1)}, bf16[512,1024]{1,0:T(8,128)(2,1)}, u32[]{:S(2)}) copy-start(bf16[512,1024]{1,0:T(8,128)(2,1)} %param.27) | copy-start | bytes 3145732
  547.5 25.4 %copy-start.27 = (f32[1,1024]{1,0:T(1,128)S(1)}, f32[1,1024]{1,0:T(1,128)}, u32[]{:S(2)}) copy-start(f32[1,1024]{1,0:T(1,128)} %copy-done.26) | copy-start | bytes 12292
  547.5 25.4 %copy-start.29 = (f32[1,1024]{1,0:T(1,128)S(1)}, f32[1,1024]{1,0:T(1,128)}, u32[]{:S(2)}) copy-start(f32[1,1024]{1,0:T(1,128)} %copy-done.28) | copy-start | bytes 12292
  547.5 25.4 %copy-start.31 = (f32[512]{0:T(512)S(1)}, f32[512]{0:T(512)}, u32[]{:S(2)}) copy-start(f32[512]{0:T(512)} %copy-done.30) | copy-start | bytes 6148
  547.6 28.0 %copy-start.37 = (f32[512]{0:T(512)S(1)}, f32[512]{0:T(512)}, u32[]{:S(2)}) copy-start(f32[512]{0:T(512)} %copy-done.36) | copy-start | bytes 6148
  547.6 28.0 %copy-start.35 = (f32[512]{0:T(512)S(1)}, f32[512]{0:T(512)}, u32[]{:S(2)}) copy-start(f32[512]{0:T(512)} %copy-done.34) | copy-start | bytes 6148
  547.6 31.4 %copy-start.39 = (f32[512]{0:T(512)S(1)}, f32[512]{0:T(512)}, u32[]{:S(2)}) copy-start(f32[512]{0:T(512)} %copy-done.38) | copy-start | bytes 6148
  547.6 31.4 %copy-start.40 = (f32[1,1024]{1,0:T(1,128)S(1)}, f32[1,1024]{1,0:T(1,128)}, u32[]{:S(2)}) copy-start(f32[1,1024]{1,0:T(1,128)} %get-tuple-element.411) | copy-start | bytes 12292
  547.6 31.4 %copy-start.41 = (f32[1,1024]{1,0:T(1,128)S(1)}, f32[1,1024]{1,0:T(1,128)}, u32[]{:S(2)}) copy-start(f32[1,1024]{1,0:T(1,128)} %get-tuple-element.414) | copy-start | bytes 12292
  579.0 47.5 %copy-start.33 = (f32[6,1024]{1,0:T(8,128)S(1)}, f32[6,1024]{1,0:T(8,128)}, u32[]{:S(2)}) copy-start(f32[6,1024]{1,0:T(8,128)} %param.43) | copy-start | bytes 73732
  583.7 192.3 %copy-start.17 = (f32[24,128,128]{2,1,0:T(8,128)S(1)}, f32[24,128,128]{2,1,0:T(8,128)}, u32[]{:S(2)}) copy-start(f32[24,128,128]{2,1,0:T(8,128)} %param.40) | copy-start | bytes 4718596
  774.4 5.6 copy-start.3
  776.1 4.0 copy-start.18
  780.0 4.6 copy-start.19
  (22 other events, 50.7 us)
Sparse Core Ops, SparseCore 0:
  10.2 52.4 all-gather.8
  64.8 33.4 all-gather.6
  100.4 34.4 all-gather.16
  136.9 49.6 all-gather.12
  188.6 32.9 all-gather.10
  223.5 51.0 all-gather.14
  394.0 44.6 reduce-scatter.8
  441.8 44.8 reduce-scatter.6
  489.3 71.7 reduce-scatter.4
  564.9 207.9 reduce-scatter.10
where the time goes:
time: 800 us; the launch traced here: 795 us
  matrix products  222 us (28%)
  waiting for transfers between devices  190 us (24%)
  local copies, waits for them, and re-layouts  152 us (19%)
  other arithmetic  102 us (13%)
  blocking collectives  97.4 us (12%)
  between operations  15.2 us (2%)
  loops' own time  14.1 us (2%)
    reduce_scatter x1, waiting for transfers between devices, shards(): lax.psum_scatter(ordered, 'dp', scatter_dimension=0, tiled=True)  146 us
    psum x1, blocking collectives, shards(): row_total = lax.psum(row_partial, ('dp', 'tensor'))  42.7 us
    all_gather x1, waiting for transfers between devices, shards(): lax.all_gather(normed_attn.astype(jnp.bfloat16), 'tensor', axis=0, tiled=...  35.6 us
    all_gather x1, blocking collectives, shards(): lax.all_gather(dense_weight, 'dp', axis=1, tiled=True)  33.2 us
    dot_general x8, matrix products, block_scores(): jnp.einsum('qhd,khd->hqk', query_block, keys_seq, preferred_element_type=...  29.6 us
    dot_general x1, matrix products, shards(): jnp.einsum('rd,fd->rf', all_grad, back_fc2, preferred_element_type=jnp.fl...  27.8 us
    dot_general x4, matrix products, back_block(): jnp.einsum('qhd,khd->hqk', grad_block, values_seq, preferred_element_type...  27.7 us
    dot_general x4, matrix products, back_block(): jnp.einsum('hqk,qhd->khd', probabilities.astype(jnp.bfloat16), grad_block...  23.7 us
  transfers between devices with their start and end apart: 10, of which 3 were waited for; matrix products, arithmetic and copies ran while one was open for 56% of the time, Pallas kernels for 0%

commit v1 on v0

v1 whole, which is shorter than its diff:
```python
import functools
import math

import jax
import jax.numpy as jnp
import numpy as np
from jax import lax
from jax.experimental import pallas as pl
from jax.experimental.pallas import tpu as pltpu
from jax.sharding import PartitionSpec as P

HEAD = 64
ROT = 16
LEN = 1024
BLOCK = 128
TILE = 256
MESH = pl.DeviceIdType.MESH
VMEM_LIMIT = 60 * 1024 * 1024

highest = lax.Precision.HIGHEST
masked_score = -1e30
shampoo_rate = 0.03
adagrad_rate = 0.1
stat_decay = 0.5
f32 = jnp.float32
bf16 = jnp.bfloat16


def adagrad_step(grad_vec, accum):
    accum_next = accum + grad_vec * grad_vec
    return (accum_next, -adagrad_rate * grad_vec * lax.rsqrt(accum_next))


def rotary_wide():
    half = ROT // 2
    inverse = np.power(np.float32(10000.0), -(np.arange(half, dtype=np.float32) * np.float32(2.0 / ROT)))
    angles = np.arange(LEN, dtype=np.float32)[:, None] * inverse.astype(np.float32)[None, :]
    cosine, sine = np.cos(angles), np.sin(angles)
    rest = HEAD - ROT
    cos_one = np.concatenate([cosine, cosine, np.ones((LEN, rest), np.float32)], axis=1)
    sin_one = np.concatenate([-sine, sine, np.zeros((LEN, rest), np.float32)], axis=1)
    wide = np.concatenate([cos_one, cos_one, sin_one, sin_one], axis=1)
    return wide.astype(np.float32)


def ring_place(me, count):
    low, high = me % 2, me // 2
    return low * (count - 1 - high) + (1 - low) * high


def ring_device(place, count):
    upper = place // (count // 2)
    return (1 - upper) * (2 * place) + upper * (2 * (count - 1 - place) + 1)


def hop_count(half, way, count):
    far = count // 2
    return far if half == way else far - 1


def for_hops(first, last, body, count):
    if count <= 8:
        for hop in range(first, last):
            body(hop)
    elif last > first:

        @pl.loop(first, last)
        def _(hop):
            body(hop)


class Ring:
    def __init__(self, count):
        self.count = count
        self.me = lax.axis_index("dp")
        self.tensor = lax.axis_index("tensor")
        self.place = ring_place(self.me, count)
        self.peer = [
            (ring_device((self.place + step) % count, count), self.tensor) for step in (1, count - 1)
        ]

    def at(self, offset):
        return ring_device((self.place + offset + 2 * self.count) % self.count, self.count)


class Gather:
    def __init__(self, ring, locals_, fulls, send, recv):
        self.ring, self.locals, self.fulls, self.send, self.recv = ring, locals_, fulls, send, recv
        self.far = ring.count // 2

    def part(self, ref, w, half, owner=None):
        rows, cols = self.locals[w].shape
        base = 0 if owner is None else owner * rows
        if rows % 32 == 0:
            return ref.at[pl.ds(pl.multiple_of(base + half * (rows // 2), 16), rows // 2)]
        return ref.at[pl.ds(base, rows), pl.ds(half * (cols // 2), cols // 2)]

    def sem(self, w, half, way, hop):
        return ((w * 2 + half) * 2 + way) * self.far + hop - 1

    def copy(self, w, half, way, hop, source):
        owner = self.ring.at((1 - hop) if way == 0 else (hop - 1))
        src = self.part(self.locals[w], w, half) if source else self.part(self.fulls[w], w, half, owner)
        return pltpu.make_async_remote_copy(
            src_ref=src,
            dst_ref=self.part(self.fulls[w], w, half, owner),
            send_sem=self.send.at[self.sem(w, half, way, hop)],
            recv_sem=self.recv.at[self.sem(w, half, way, hop)],
            device_id=self.ring.peer[way],
            device_id_type=MESH,
        )

    def arrival(self, w, half, way, hop):
        owner = self.ring.at(-hop if way == 0 else hop)
        dst = self.part(self.fulls[w], w, half, owner)
        return pltpu.make_async_remote_copy(
            src_ref=dst,
            dst_ref=dst,
            send_sem=self.send.at[self.sem(w, half, way, hop)],
            recv_sem=self.recv.at[self.sem(w, half, way, hop)],
            device_id=self.ring.peer[way],
            device_id_type=MESH,
        )

    def begin(self, w):
        for half in range(2):
            for way in range(2):
                if hop_count(half, way, self.ring.count) >= 1:
                    self.copy(w, half, way, 1, True).start()

    def forward(self, w, hop, last):
        for half in range(2):
            for way in range(2):
                hops = self.far if half == way else self.far - 1
                if last and hops != self.far:
                    continue
                self.arrival(w, half, way, hop).wait_recv()
                if not last:
                    more = self.far if half == way else self.far - 1
                    if more == self.far:
                        self.copy(w, half, way, hop + 1, False).start()
                    else:

                        @pl.when(hop + 1 <= more)
                        def _():
                            self.copy(w, half, way, hop + 1, False).start()

    def finish(self, w):
        for half in range(2):
            for way in range(2):
                hops = hop_count(half, way, self.ring.count)
                if hops >= 1:
                    self.copy(w, half, way, 1, True).wait_send()
                for_hops(
                    2, hops + 1, lambda hop: self.copy(w, half, way, hop, False).wait_send(), self.ring.count
                )


class Rows:
    def __init__(self, local, full, send, recv, own):
        self.tensor = lax.axis_index("tensor")
        self.dp = lax.axis_index("dp")
        self.near = self.tensor + 1 - 2 * (self.tensor % 2)
        self.across = (self.tensor + 2) % 4
        self.local, self.full, self.send, self.recv, self.own = local, full, send, recv, own
        self.rows = local.shape[0]

    def slot(self, owner, piece=None):
        if piece is None:
            return self.full.at[pl.ds(pl.multiple_of(owner * self.rows, 16), self.rows)]
        half = self.rows // 2
        return self.full.at[pl.ds(pl.multiple_of(owner * self.rows + piece * half, 16), half)]

    def remote(self, src, dst, sem, device):
        return pltpu.make_async_remote_copy(
            src_ref=src,
            dst_ref=dst,
            send_sem=self.send.at[sem],
            recv_sem=self.recv.at[sem],
            device_id=(self.dp, device),
            device_id_type=MESH,
        )

    def keep(self):
        return pltpu.make_async_copy(self.local, self.slot(self.tensor), self.own)

    def pair(self):
        return self.remote(self.local, self.slot(self.tensor), 0, self.near)

    def cross(self, piece):
        half = self.rows // 2
        return self.remote(
            self.local.at[pl.ds(piece * half, half)], self.slot(self.tensor, piece), 1 + piece, self.across
        )

    def onward(self, piece):
        here = self.slot(self.across, piece)
        return self.remote(here, here, 3 + piece, self.near)

    def begin_near(self):
        self.keep().start()
        self.pair().start()

    def begin_cross(self):
        for piece in range(2):
            self.cross(piece).start()

    def pass_on(self):
        for piece in range(2):
            self.cross(piece).wait_recv()
            self.onward(piece).start()

    def finish(self):
        self.keep().wait()
        self.pair().wait()
        for piece in range(2):
            self.cross(piece).wait_send()
            self.onward(piece).wait()


def greet(devices):
    barrier = pltpu.get_barrier_semaphore()
    for device in devices:
        pl.semaphore_signal(barrier, inc=1, device_id=device, device_id_type=MESH)
    pl.semaphore_wait(barrier, len(devices))


def gather_kernel(count, x, dy, wq, wd, w1, w2, xf, dyf, wqf, wdf, w1f, w2f, rs, rr, ro, gs, gr, go):
    ring = Ring(count)
    locals_, fulls = (wq, wd, w1, w2), (wqf, wdf, w1f, w2f)
    gather = Gather(ring, locals_, fulls, gs, gr)
    rx = Rows(x, xf, rs.at[0], rr.at[0], ro.at[0])
    ry = Rows(dy, dyf, rs.at[1], rr.at[1], ro.at[1])
    greet([ring.peer[0], ring.peer[1], (ring.me, rx.near), (ring.me, rx.across)])
    gather.begin(0)
    rx.begin_cross()
    rx.begin_near()
    ry.begin_near()
    own = []
    for w in range(4):
        rows = locals_[w].shape[0]
        own.append(
            pltpu.make_async_copy(
                locals_[w], fulls[w].at[pl.ds(pl.multiple_of(ring.me * rows, 16), rows)], go.at[w]
            )
        )
        own[-1].start()
    far = count // 2
    for w in range(4):
        for_hops(1, far, lambda hop: gather.forward(w, hop, False), count)
        if w < 3:
            gather.begin(w + 1)
        gather.forward(w, far, True)
        if w == 1:
            rx.pass_on()
            ry.begin_cross()
    ry.pass_on()
    for w in range(4):
        gather.finish(w)
        own[w].wait()
    rx.finish()
    ry.finish()


def gather_all(count, x, dy, wq, wd, w1, w2):
    far = count // 2
    outs = [jax.ShapeDtypeStruct((4 * v.shape[0], v.shape[1]), v.dtype) for v in (x, dy)]
    outs += [jax.ShapeDtypeStruct((count * v.shape[0], v.shape[1]), v.dtype) for v in (wq, wd, w1, w2)]
    moved = sum(v.size * 2 for v in outs)
    return pl.pallas_call(
        functools.partial(gather_kernel, count),
        out_shape=outs,
        in_specs=[pl.BlockSpec(memory_space=pl.ANY)] * 6,
        out_specs=[pl.BlockSpec(memory_space=pl.ANY)] * 6,
        scratch_shapes=[
            pltpu.SemaphoreType.DMA((2, 5)),
            pltpu.SemaphoreType.DMA((2, 5)),
            pltpu.SemaphoreType.DMA((2,)),
            pltpu.SemaphoreType.DMA((16 * far,)),
            pltpu.SemaphoreType.DMA((16 * far,)),
            pltpu.SemaphoreType.DMA((4,)),
        ],
        compiler_params=pltpu.CompilerParams(
            collective_id=0, has_side_effects=True, vmem_limit_bytes=VMEM_LIMIT
        ),
        cost_estimate=pl.CostEstimate(flops=0, bytes_accessed=moved, transcendentals=0),
        name="gather_all",
    )(x, dy, wq, wd, w1, w2)


def dot_nn(a, b):
    return lax.dot_general(a, b, (((1,), (0,)), ((), ())), preferred_element_type=f32)


def dot_nt(a, b):
    return lax.dot_general(a, b, (((1,), (1,)), ((), ())), preferred_element_type=f32)


def dot_tn(a, b):
    return lax.dot_general(a, b, (((0,), (0,)), ((), ())), preferred_element_type=f32)


def normed(x):
    average = jnp.mean(x, axis=-1, keepdims=True)
    centered = x - average
    variance = jnp.mean(centered * centered, axis=-1, keepdims=True)
    scale = lax.rsqrt(variance + 1e-05)
    return centered * scale, scale


def swap_halves(v):
    half = ROT // 2
    lane = lax.broadcasted_iota(jnp.int32, v.shape, 1) % HEAD
    return jnp.where(lane < half, pltpu.roll(v, v.shape[1] - half, 1), pltpu.roll(v, half, 1))


def attention_kernel(
    heads, lim_ref, x_ref, dy_ref, wq_ref, wd_ref, gain_ref, bias_ref, qb_ref, rot_ref,
    h1_ref, h2_ref, dyb_ref, ctx_ref, dproj_ref, sum_ref,
    qs, ks, vs, dcs, dqs, dks, dvs, ctxs,
):
    seq = pl.program_id(0)
    limit = lim_ref[seq]

    @pl.when(seq == 0)
    def _():
        sum_ref[...] = jnp.zeros_like(sum_ref)

    @pl.loop(0, LEN // TILE)
    def _(i):
        rows = pl.ds(pl.multiple_of(i * TILE, TILE), TILE)
        xhat, _ = normed(x_ref[rows, :].astype(f32))
        h1 = (xhat * gain_ref[0:1, :] + bias_ref[0:1, :]).astype(bf16)
        h1_ref[rows, :] = h1
        h2_ref[rows, :] = (xhat * gain_ref[1:2, :] + bias_ref[1:2, :]).astype(bf16)
        proj = dot_nn(h1, wq_ref[...]) + qb_ref[...]
        place = i * TILE + lax.broadcasted_iota(jnp.int32, (TILE, 1), 0)
        dy = jnp.where(place < limit, dy_ref[rows, :].astype(f32), 0.0)
        sum_ref[4:5, :] += jnp.sum(dy, axis=0, keepdims=True)
        dyb = dy.astype(bf16)
        dyb_ref[rows, :] = dyb
        dctx = dot_nn(dyb, wd_ref[...]).astype(bf16)
        cosine, sine = rot_ref[rows, 0:128], rot_ref[rows, 128:256]
        for h in range(heads):
            pair = proj[:, 3 * HEAD * h : 3 * HEAD * h + 2 * HEAD]
            pair = pair * cosine + swap_halves(pair) * sine
            qs[h, rows, :] = (pair[:, :HEAD].astype(bf16) * 0.125).astype(bf16)
            ks[h, rows, :] = pair[:, HEAD:].astype(bf16)
            vs[h, rows, :] = proj[:, 3 * HEAD * h + 2 * HEAD : 3 * HEAD * (h + 1)].astype(bf16)
            dcs[h, rows, :] = dctx[:, HEAD * h : HEAD * (h + 1)]

    @pl.loop(0, heads)
    def _(h):
        for i in reversed(range(LEN // TILE)):
            seen = (i + 1) * TILE
            rows = slice(i * TILE, seen)
            q, do = qs[h, rows, :], dcs[h, rows, :]
            k, v = ks[h, :seen, :], vs[h, :seen, :]
            s = dot_nt(q, k)
            col = lax.broadcasted_iota(jnp.int32, (TILE, seen), 1)
            row = lax.broadcasted_iota(jnp.int32, (TILE, seen), 0) + i * TILE
            s = jnp.where((col <= row) & (col < limit), s, masked_score)
            p = jnp.exp(s - jnp.max(s, axis=1, keepdims=True))
            p = p * (1.0 / jnp.sum(p, axis=1, keepdims=True))
            pb = p.astype(bf16)
            ctxs[h, rows, :] = dot_nn(pb, v).astype(bf16)
            dp = dot_nt(do, v)
            ds = (p * (dp - jnp.sum(p * dp, axis=1, keepdims=True))).astype(bf16)
            dqs[h, rows, :] = dot_nn(ds, k) * 0.125
            dv_part = dot_tn(pb, do)
            dk_part = dot_tn(ds, q)
            if i == LEN // TILE - 1:
                dvs[h, :, :] = dv_part
                dks[h, :, :] = dk_part
            else:
                dvs[h, :seen, :] += dv_part
                dks[h, :seen, :] += dk_part

    @pl.loop(0, LEN // TILE)
    def _(i):
        rows = pl.ds(pl.multiple_of(i * TILE, TILE), TILE)
        cosine, sine = rot_ref[rows, 0:128], rot_ref[rows, 128:256]
        for h in range(heads):
            pair = jnp.concatenate([dqs[h, rows, :], dks[h, rows, :]], axis=1)
            pair = (pair * cosine - swap_halves(pair) * sine).astype(bf16)
            low = dvs[h, rows, :].astype(bf16)
            lo = 3 * HEAD * h
            dproj_ref[rows, lo : lo + 2 * HEAD] = pair
            dproj_ref[rows, lo + 2 * HEAD : lo + 3 * HEAD] = low
            sum_ref[5:6, lo : lo + 2 * HEAD] += jnp.sum(pair.astype(f32), axis=0, keepdims=True)
            sum_ref[5:6, lo + 2 * HEAD : lo + 3 * HEAD] += jnp.sum(low.astype(f32), axis=0, keepdims=True)
            ctx_ref[rows, HEAD * h : HEAD * (h + 1)] = ctxs[h, rows, :]


def attention_all(limits, xf, dyf, wqf, wdf, gains, biases, qkv_bias, rot):
    seqs = limits.shape[0]
    width = xf.shape[1]
    heads = wqf.shape[1] // (3 * HEAD)

    def per_seq(cols):
        return pl.BlockSpec((LEN, cols), lambda s: (s, 0))

    def whole(shape):
        return pl.BlockSpec(shape, lambda s: (0, 0))

    out = lambda cols: jax.ShapeDtypeStruct((seqs * LEN, cols), bf16)
    per_head = lambda dtype: pltpu.VMEM((heads, LEN, HEAD), dtype)
    return pl.pallas_call(
        functools.partial(attention_kernel, heads),
        grid=(seqs,),
        out_shape=[
            out(width), out(width), out(width), out(heads * HEAD), out(heads * 3 * HEAD),
            jax.ShapeDtypeStruct((8, width), f32),
        ],
        in_specs=[
            pl.BlockSpec(memory_space=pltpu.SMEM),
            per_seq(width), per_seq(width), whole(wqf.shape), whole(wdf.shape), whole(gains.shape),
            whole(biases.shape), whole(qkv_bias.shape), whole(rot.shape),
        ],
        out_specs=[
            per_seq(width), per_seq(width), per_seq(width), per_seq(heads * HEAD),
            per_seq(heads * 3 * HEAD), whole((8, width)),
        ],
        scratch_shapes=[per_head(bf16)] * 4 + [per_head(f32)] * 3 + [per_head(bf16)],
        compiler_params=pltpu.CompilerParams(vmem_limit_bytes=VMEM_LIMIT),
        cost_estimate=pl.CostEstimate(flops=int(1e10), bytes_accessed=int(3e7), transcendentals=int(1e7)),
        name="attention_all",
    )(limits, xf, dyf, wqf, wdf, gains, biases, qkv_bias, rot)


def gelu_both(x):
    bell = jnp.exp(-0.5 * x * x)
    u = jnp.abs(x) * (1.0 / math.sqrt(2.0))
    t = 1.0 / (1.0 + 0.3275911 * u)
    poly = t * (0.254829592 + t * (-0.284496736 + t * (1.421413741 + t * (-1.453152027 + t * 1.061405429))))
    tail = 0.5 * poly * bell
    phi = jnp.where(x < 0.0, tail, 1.0 - tail)
    return x * phi, phi + x * bell * (1.0 / math.sqrt(2.0 * math.pi))


def rows_kernel(
    x_ref, h2_ref, dyb_ref, ctx_ref, dproj_ref, wq_ref, wd_ref, w1_ref, w2_ref, gain_ref, fb_ref,
    act_ref, dab_ref, br_ref, e_ref, sum_ref,
):
    @pl.when(pl.program_id(0) == 0)
    def _():
        sum_ref[...] = jnp.zeros_like(sum_ref)

    pre = dot_nn(h2_ref[...], w1_ref[...]) + fb_ref[...]
    act, slope = gelu_both(pre)
    act = act.astype(bf16)
    act_ref[...] = act
    dab = (dot_nn(dyb_ref[...], w2_ref[...]) * slope).astype(bf16)
    dab_ref[...] = dab
    br_ref[...] = (dot_nt(ctx_ref[...], wd_ref[...]) + dot_nt(act, w2_ref[...])).astype(bf16)
    dh2 = dot_nt(dab, w1_ref[...])
    dh1 = dot_nt(dproj_ref[...], wq_ref[...])
    xhat, _ = normed(x_ref[...].astype(f32))
    e_ref[...] = (dh1 * gain_ref[0:1, :] + dh2 * gain_ref[1:2, :]).astype(bf16)
    total = lambda v: jnp.sum(v, axis=0, keepdims=True)
    sum_ref[0:1, :] += total(dh1 * xhat)
    sum_ref[1:2, :] += total(dh2 * xhat)
    sum_ref[2:3, :] += total(dh1)
    sum_ref[3:4, :] += total(dh2)
    sum_ref[6:7, :] += total(dab.astype(f32))


def rows_all(xf, h2, dyb, ctx, dproj, wqf, wdf, w1f, w2f, gains, fc1_bias):
    rows, width = xf.shape

    def tile(cols):
        return pl.BlockSpec((TILE, cols), lambda s: (s, 0))

    def whole(v):
        return pl.BlockSpec(v.shape, lambda s: (0, 0))

    out = lambda cols: jax.ShapeDtypeStruct((rows, cols), bf16)
    hidden = w1f.shape[1]
    return pl.pallas_call(
        rows_kernel,
        grid=(rows // TILE,),
        out_shape=[out(hidden), out(hidden), out(width), out(width), jax.ShapeDtypeStruct((8, width), f32)],
        in_specs=[tile(v.shape[1]) for v in (xf, h2, dyb, ctx, dproj)]
        + [whole(v) for v in (wqf, wdf, w1f, w2f, gains, fc1_bias)],
        out_specs=[tile(hidden), tile(hidden), tile(width), tile(width), pl.BlockSpec((8, width), lambda s: (0, 0))],
        compiler_params=pltpu.CompilerParams(vmem_limit_bytes=VMEM_LIMIT),
        cost_estimate=pl.CostEstimate(flops=int(2e10), bytes_accessed=int(3e7), transcendentals=int(4e6)),
        name="rows_all",
    )(xf, h2, dyb, ctx, dproj, wqf, wdf, w1f, w2f, gains, fc1_bias)


def weights_kernel(plan, h1_ref, ctx_ref, h2_ref, act_ref, dproj_ref, dyb_ref, dab_ref, g_ref):
    job = pl.program_id(0)
    lefts = (h1_ref, ctx_ref, h2_ref, act_ref)
    rights = (dproj_ref, dyb_ref, dab_ref, dyb_ref)
    for kind, (first, jobs, base, per_row) in enumerate(plan):

        @pl.when((job >= first) & (job < first + jobs))
        def _():
            grad = dot_tn(lefts[kind][...], rights[kind][...]).astype(bf16)
            start = base + (job - first) * (TILE // BLOCK) * per_row
            for r in range(TILE // BLOCK):
                for c in range(per_row):
                    g_ref[start + r * per_row + c] = grad[
                        r * BLOCK : (r + 1) * BLOCK, c * BLOCK : (c + 1) * BLOCK
                    ]


def weights_all(h1, ctx, h2, act, dproj, dyb, dab):
    rows = h1.shape[0]
    lefts, rights = (h1, ctx, h2, act), (dproj, dyb, dab, dyb)
    plan, first, base = [], 0, 0
    for left, right in zip(lefts, rights):
        jobs, per_row = left.shape[1] // TILE, right.shape[1] // BLOCK
        plan.append((first, jobs, base, per_row))
        first, base = first + jobs, base + jobs * (TILE // BLOCK) * per_row

    def tile(kind):
        begin, jobs = plan[kind][:2]
        return pl.BlockSpec((rows, TILE), lambda j: (0, jnp.clip(j - begin, 0, jobs - 1)))

    def whole(v):
        return pl.BlockSpec(v.shape, lambda j: (0, 0))

    return pl.pallas_call(
        functools.partial(weights_kernel, tuple(plan)),
        grid=(first,),
        out_shape=jax.ShapeDtypeStruct((base, BLOCK, BLOCK), bf16),
        in_specs=[tile(k) for k in range(4)] + [whole(dproj), whole(dyb), whole(dab)],
        out_specs=pl.BlockSpec((base, BLOCK, BLOCK), lambda j: (0, 0, 0)),
        compiler_params=pltpu.CompilerParams(vmem_limit_bytes=VMEM_LIMIT),
        cost_estimate=pl.CostEstimate(flops=int(1.3e10), bytes_accessed=int(3e7), transcendentals=0),
        name="weights_all",
    )(h1, ctx, h2, act, dproj, dyb, dab)


class Scatter:
    def __init__(self, ring, order, blocks, out, sbuf, rbuf, send, recv):
        self.ring, self.order, self.blocks, self.out = ring, order, blocks, out
        self.sbuf, self.rbuf, self.send, self.recv = sbuf, rbuf, send, recv
        self.per = out.shape[0]
        self.far = ring.count // 2

    def index(self, half, way, hop):
        return (half * 2 + way) * self.far + hop - 1

    def copy(self, half, way, hop):
        i = self.index(half, way, hop)
        return pltpu.make_async_remote_copy(
            src_ref=self.sbuf.at[i],
            dst_ref=self.rbuf.at[i],
            send_sem=self.send.at[i],
            recv_sem=self.recv.at[i],
            device_id=self.ring.peer[way],
            device_id_type=MESH,
        )

    def own(self, dest, half, k):
        return self.blocks[self.order[dest * self.per + k], half * 64 : half * 64 + 64, :].astype(f32)

    def step(self, half, way, hop, hops, first):
        dest = self.ring.at((hops + 1 - hop) if way == 0 else (hop - hops - 1))
        i = self.index(half, way, hop)
        if not first:
            self.copy(half, way, hop - 1).wait_recv()

        def one(k, carry):
            value = self.own(dest, half, k)
            if not first:
                value = value + self.rbuf[i - 1, k].astype(f32)
            self.sbuf[i, k] = value.astype(bf16)
            return carry

        lax.fori_loop(0, self.per, one, 0)
        self.copy(half, way, hop).start()

    def last(self, half, scale):
        came = []
        for way in range(2):
            hops = hop_count(half, way, self.ring.count)
            if hops >= 1:
                self.copy(half, way, hops).wait_recv()
                came.append(self.index(half, way, hops))
        me = self.ring.me

        def one(k, carry):
            value = self.own(me, half, k)
            for i in came:
                value = value + self.rbuf[i, k].astype(f32)
            self.out[k, half * 64 : half * 64 + 64, :] = value * scale
            return carry

        lax.fori_loop(0, self.per, one, 0)

    def finish(self):
        for half in range(2):
            for way in range(2):
                hops = hop_count(half, way, self.ring.count)
                for_hops(1, hops + 1, lambda hop: self.copy(half, way, hop).wait_send(), self.ring.count)


class RowSum:
    def __init__(self, part, out, r1, s2, r2, send, recv):
        self.tensor = lax.axis_index("tensor")
        self.dp = lax.axis_index("dp")
        self.near = self.tensor + 1 - 2 * (self.tensor % 2)
        self.across = (self.tensor + 2) % 4
        self.part, self.out, self.r1, self.s2, self.r2 = part, out, r1, s2, r2
        self.send, self.recv = send, recv
        self.rows = out.shape[0]

    def slot(self, owner):
        return self.part.at[pl.ds(pl.multiple_of(owner * self.rows, 16), self.rows)]

    def remote(self, src, dst, sem, device):
        return pltpu.make_async_remote_copy(
            src_ref=src, dst_ref=dst, send_sem=self.send.at[sem], recv_sem=self.recv.at[sem],
            device_id=(self.dp, device), device_id_type=MESH,
        )

    def pair(self, k):
        owner = (self.near + 2) % 4 if k == 0 else self.near
        return self.remote(self.slot(owner), self.r1.at[k], k, self.near)

    def cross(self):
        return self.remote(self.s2, self.r2, 2, self.across)

    def begin(self):
        self.pair(0).start()
        self.pair(1).start()

    def middle(self):
        self.pair(0).wait_recv()
        self.s2[...] = (self.slot(self.across)[...].astype(f32) + self.r1[0].astype(f32)).astype(bf16)
        self.cross().start()

    def end(self):
        self.pair(1).wait_recv()
        self.cross().wait_recv()
        self.out[...] = (
            self.slot(self.tensor)[...].astype(f32) + self.r1[1].astype(f32) + self.r2[...].astype(f32)
        )
        self.pair(0).wait_send()
        self.pair(1).wait_send()
        self.cross().wait_send()


def sums_kernel(
    count, scale, order, blocks, br, e, small, grad, br_sum, e_sum, small_sum,
    sbuf, rbuf, r1, s2, r2, t_in, d_in, d_out, ss, sr, rs, rr, ts, tr, ds, dr,
):
    ring = Ring(count)
    me, tensor = ring.me, ring.tensor
    scatter = Scatter(ring, order, blocks, grad, sbuf, rbuf, ss, sr)
    sums = [
        RowSum(part, out, r1.at[n], s2.at[n], r2.at[n], rs.at[n], rr.at[n])
        for n, (part, out) in enumerate(((br, br_sum), (e, e_sum)))
    ]

    def t_copy(step):
        return pltpu.make_async_remote_copy(
            src_ref=small, dst_ref=t_in.at[tensor], send_sem=ts.at[step], recv_sem=tr.at[step],
            device_id=(me, (tensor + step) % 4), device_id_type=MESH,
        )

    def d_copy(step):
        return pltpu.make_async_remote_copy(
            src_ref=d_out, dst_ref=d_in.at[me], send_sem=ds.at[step], recv_sem=dr.at[step],
            device_id=((me + step) % count, tensor), device_id_type=MESH,
        )

    barrier = pltpu.get_barrier_semaphore()
    for step in range(1, 4):
        pl.semaphore_signal(barrier, inc=1, device_id=(me, (tensor + step) % 4), device_id_type=MESH)

    @pl.loop(1, count)
    def _(step):
        pl.semaphore_signal(barrier, inc=1, device_id=((me + step) % count, tensor), device_id_type=MESH)

    pl.semaphore_wait(barrier, 3 + count - 1)

    far = count // 2
    for half in range(2):
        for way in (half, 1 - half):
            hops = hop_count(half, way, count)
            if hops >= 1:
                scatter.step(half, way, 1, hops, True)
    for step in range(1, 4):
        t_copy(step).start()
    for s in sums:
        s.begin()
    sums[0].middle()
    for step in range(1, 4):
        t_copy(step).wait_recv()
    t_in[tensor] = small[...]
    row = lax.broadcasted_iota(jnp.int32, small.shape, 0)
    total = t_in[0] + t_in[1] + t_in[2] + t_in[3]
    d_out[...] = jnp.where(row < 4, total, small[...])

    @pl.loop(1, count)
    def _(step):
        d_copy(step).start()

    def ring_step(hop):
        for half in range(2):
            for way in (half, 1 - half):
                hops = hop_count(half, way, count)
                if half == way:
                    scatter.step(half, way, hop, hops, False)
                else:

                    @pl.when(hop <= hops)
                    def _():
                        scatter.step(half, way, hop, hops, False)

    for_hops(2, far, ring_step, count)
    sums[1].middle()
    if far >= 2:
        ring_step(far)
    sums[0].end()

    @pl.loop(1, count)
    def _(step):
        d_copy(step).wait_recv()

    d_in[me] = d_out[...]
    small_sum[...] = lax.fori_loop(1, count, lambda k, acc: acc + d_in[k], d_in[0])
    sums[1].end()
    for half in range(2):
        scatter.last(half, scale)
    scatter.finish()
    for step in range(1, 4):
        t_copy(step).wait_send()

    @pl.loop(1, count)
    def _(step):
        d_copy(step).wait_send()


def sums_all(count, scale, order, blocks, br, e, small):
    per = blocks.shape[0] // count
    rows, width = br.shape[0] // 4, br.shape[1]
    far = count // 2
    vmem = pl.BlockSpec(memory_space=pltpu.VMEM)
    dma = lambda *n: pltpu.SemaphoreType.DMA(n)
    return pl.pallas_call(
        functools.partial(sums_kernel, count, scale),
        out_shape=[
            jax.ShapeDtypeStruct((per, BLOCK, BLOCK), f32),
            jax.ShapeDtypeStruct((rows, width), f32),
            jax.ShapeDtypeStruct((rows, width), f32),
            jax.ShapeDtypeStruct(small.shape, f32),
        ],
        in_specs=[pl.BlockSpec(memory_space=pltpu.SMEM)] + [vmem] * 4,
        out_specs=[vmem] * 4,
        scratch_shapes=[
            pltpu.VMEM((4 * far, per, 64, BLOCK), bf16),
            pltpu.VMEM((4 * far, per, 64, BLOCK), bf16),
            pltpu.VMEM((2, 2, rows, width), bf16),
            pltpu.VMEM((2, rows, width), bf16),
            pltpu.VMEM((2, rows, width), bf16),
            pltpu.VMEM((4,) + small.shape, f32),
            pltpu.VMEM((count,) + small.shape, f32),
            pltpu.VMEM(small.shape, f32),
            dma(4 * far), dma(4 * far), dma(2, 3), dma(2, 3), dma(4), dma(4), dma(count), dma(count),
        ],
        compiler_params=pltpu.CompilerParams(
            collective_id=1, has_side_effects=True, vmem_limit_bytes=VMEM_LIMIT
        ),
        cost_estimate=pl.CostEstimate(flops=0, bytes_accessed=int(3e7), transcendentals=0),
        name="sums_all",
    )(order, blocks, br, e, small)


def shards(
    tokens, out_grad, seq_lengths, norm_gains, row_biases, qkv_weight, qkv_bias, dense_weight, fc1_weight,
    fc1_bias, fc2_weight, block_slot, left_stat, right_stat, left_root, right_root, row_accum,
    qkv_bias_accum, fc1_bias_accum,
):
    tensor_count = lax.axis_size("tensor")
    dp_count = lax.axis_size("dp")
    tensor_rank = lax.axis_index("tensor")
    own_rows, width = tokens.shape
    group_rows = own_rows * tensor_count
    group_seqs = seq_lengths.shape[0]
    grad_scale = 1.0 / math.sqrt(group_rows * dp_count)
    blocks_tensor = block_slot.shape[0] // tensor_count
    per_dev = blocks_tensor // dp_count

    my_slots = lax.dynamic_slice_in_dim(block_slot, tensor_rank * blocks_tensor, blocks_tensor)
    position = my_slots // per_dev // tensor_count * per_dev + my_slots % per_dev
    places = jnp.arange(blocks_tensor, dtype=jnp.int32)
    order = jnp.sum(jnp.where(position[:, None] == places[None, :], places[:, None], 0), axis=0)

    xf, dyf, wqf, wdf, w1f, w2f = gather_all(
        dp_count, tokens, out_grad, qkv_weight, dense_weight.T, fc1_weight, fc2_weight.T
    )
    h1, h2, dyb, ctx, dproj, sum_a = attention_all(
        seq_lengths, xf, dyf, wqf, wdf, norm_gains, row_biases, qkv_bias[None], jnp.asarray(rotary_wide())
    )
    act, dab, br, e, sum_b = rows_all(
        xf, h2, dyb, ctx, dproj, wqf, wdf, w1f, w2f, norm_gains, fc1_bias[None]
    )
    blocks = weights_all(h1, ctx, h2, act, dproj, dyb, dab)
    own_grad, branch, e_sum, small = sums_all(dp_count, grad_scale, order, blocks, br, e, sum_a + sum_b)

    inputs = tokens.astype(f32)
    layer_out = (inputs + branch + row_biases[2] + row_biases[3]).astype(bf16)
    row_ids = tensor_rank * own_rows + jnp.arange(own_rows)
    seq_match = (row_ids // LEN)[:, None] == jnp.arange(group_seqs)[None, :]
    row_limit = jnp.sum(jnp.where(seq_match, seq_lengths[None, :], 0), axis=1)
    row_valid = (row_ids % LEN < row_limit).astype(f32)
    grad_out = out_grad.astype(f32) * row_valid[:, None]
    xhat, scale = normed(inputs)
    input_grad = grad_out + scale * (
        e_sum
        - jnp.mean(e_sum, axis=-1, keepdims=True)
        - xhat * jnp.mean(e_sum * xhat, axis=-1, keepdims=True)
    )

    left_next = stat_decay * left_stat + (1.0 - stat_decay) * jnp.einsum(
        "sij,skj->sik", own_grad, own_grad, precision=highest
    )
    right_next = stat_decay * right_stat + (1.0 - stat_decay) * jnp.einsum(
        "sji,sjk->sik", own_grad, own_grad, precision=highest
    )
    pushed = jnp.einsum("sij,sjk->sik", left_root, own_grad, precision=highest)
    change = -shampoo_rate * jnp.einsum("sij,sjk->sik", pushed, right_root, precision=highest)

    small = small * grad_scale
    row_grads = jnp.concatenate([small[:5], small[4:5]], axis=0)
    row_next, row_change = adagrad_step(row_grads, row_accum)
    qkv_next, qkv_change = adagrad_step(small[5, : qkv_bias.shape[0]], qkv_bias_accum)
    fc1_next, fc1_change = adagrad_step(small[6, : fc1_bias.shape[0]], fc1_bias_accum)
    return (
        layer_out, input_grad, own_grad, left_next, right_next, change,
        row_next, row_change, qkv_next, qkv_change, fc1_next, fc1_change,
    )


def solution(mesh):
    both = ("dp", "tensor")
    return jax.shard_map(
        shards,
        mesh=mesh,
        in_specs=(
            P(both, None), P(both, None), P("dp"), P(), P(), P("dp", "tensor"), P("tensor"),
            P("tensor", "dp"), P("dp", "tensor"), P("tensor"), P("tensor", "dp"), P(),
            P(both, None, None), P(both, None, None), P(both, None, None), P(both, None, None),
            P(), P("tensor"), P("tensor"),
        ),
        out_specs=(
            P(both, None), P(both, None), P(both, None, None), P(both, None, None),
            P(both, None, None), P(both, None, None), P(), P(), P("tensor"), P("tensor"),
            P("tensor"), P("tensor"),
        ),
        check_vma=False,
    )
```

time: 800 us -> 321 us (0.40)
  Pallas kernels: 0 us -> 291 us
  matrix products: 222 us -> 13 us
  waiting for transfers between devices: 190 us -> 0 us
  local copies, waits for them, and re-layouts: 152 us -> 5.29 us
  blocking collectives: 97.4 us -> 0 us
  other arithmetic: 102 us -> 11.4 us
  between operations: 15.2 us -> 0.85 us
  loops' own time: 14.1 us -> 0 us
    pallas_call x0 -> x5, Pallas kernels: none -> 291 us  [the longest x1 92.9 us: gather_all(): pl.pallas_call(functools.partial(gather_kernel, count), out_shape=outs, i...]
    dot_general x40 -> x0, matrix products: 210 us -> none  [the longest x8 29.6 us: block_scores(): jnp.einsum('qhd,khd->hqk', query_block, keys_seq, preferred_element_type=...]
    reduce_scatter x4 -> x0, waiting for transfers between devices: 146 us -> none  [the longest x1 146 us: shards(): lax.psum_scatter(ordered, 'dp', scatter_dimension=0, tiled=True)]
    psum x2 -> x0, blocking collectives: 64.3 us -> none  [the longest x1 42.7 us: shards(): row_total = lax.psum(row_partial, ('dp', 'tensor'))]
    all_gather x6 -> x0, waiting for transfers between devices: 42.1 us -> none  [the longest x1 35.6 us: shards(): lax.all_gather(normed_attn.astype(jnp.bfloat16), 'tensor', axis=0, tiled=...]
    while x67 -> x0, local copies, waits for them, and re-layouts: 34.8 us -> none  [the longest x4 16.4 us: shards(): lax.map(backward_seq, (queries, keys_all, values, seq_lengths, context_gr...]
    all_gather x1 -> x0, blocking collectives: 33.2 us -> none  [shards(): lax.all_gather(dense_weight, 'dp', axis=1, tiled=True)]
    convert_element_type x8 -> x1, other arithmetic: 31.4 us -> 0.01 us  [shards(): row_valid = (row_ids % LEN < row_limit).astype(f32)]
  transfers between devices with their start and end apart: 10 -> 0, of which waited for: 3 -> 0; matrix products, arithmetic and copies ran while one was open for 56% -> 0% of each run, Pallas kernels for 0% -> 0%
where the time goes in v1:
time: 321 us
  Pallas kernels  291 us (91%)
  matrix products  13 us (4%)
  other arithmetic  11.4 us (4%)
  local copies, waits for them, and re-layouts  5.29 us (2%)
    pallas_call x1, Pallas kernels, gather_all(): pl.pallas_call(functools.partial(gather_kernel, count), out_shape=outs, i...  92.9 us
    pallas_call x1, Pallas kernels, sums_all(): pl.pallas_call(functools.partial(sums_kernel, count, scale), out_shape=[j...  79.5 us
    pallas_call x1, Pallas kernels, attention_all(): pl.pallas_call(functools.partial(attention_kernel, heads), grid=(seqs,),...  60.5 us
    pallas_call x1, Pallas kernels, rows_all(): pl.pallas_call(rows_kernel, grid=(rows // TILE,), out_shape=[out(hidden),...  32.8 us
    pallas_call x1, Pallas kernels, weights_all(): pl.pallas_call(functools.partial(weights_kernel, tuple(plan)), grid=(firs...  24.8 us

profile of v1, /device:TPU:0, one launch (start us, length us, event | category | flops | bytes accessed | tf_op | source)
XLA Modules:
  0.0 321.1 jit_solution(18260013050797020792)
XLA Ops:
  0.6 0.0 copy-start
  0.7 0.0 copy-start.11
  0.7 1.9 copy.36
  2.6 1.6 copy.35
  4.2 92.9 %gather_all.1 = (bf16[2048,1024]{1,0:T(8,128)(2,1)}, bf16[2048,1024]{1,0:T(8,128)(2,1)}, bf16[1024,768]{1,0:T(8,128)(2,1)}, bf16[1024,256]{1,0:T(8,128)(2,1)}, b...) custom-call(bf16[512,1024]{1,0:T(8,128)(2,1)} %x.1, bf16[512,1024]{1,0:T(8,128)(2,1)} %dy.1, bf16[128,768]{1,0:T(8,128)(2,1)} %wq.1, ...), custom_call_target="tpu_custom_call" | custom-call | bytes 14680064 | tf_op jit(solution)/shard_map/gather_all/pallas_call | solution.py:270
  97.0 0.0 copy-done.11
  97.1 0.6 broadcast_in_dim.43.qb_ref
  97.6 60.5 %attention_all.1 = (bf16[2048,1024]{1,0:T(8,128)(2,1)}, bf16[2048,1024]{1,0:T(8,128)(2,1)}, bf16[2048,1024]{1,0:T(8,128)(2,1)}, bf16[2048,256]{1,0:T(8,128)(2,1)...) custom-call(s32[2]{0:T(128)} %lim_ref.1, bf16[2048,1024]{1,0:T(8,128)(2,1)} %get-tuple-element.33.x_ref, ...), custom_call_target="tpu_custom_call" | custom-call | flops 10000000000 | bytes 30000000 | tf_op jit(solution)/shard_map/attention_all/pallas_call | solution.py:408
  158.2 0.0 copy-start.7
  158.2 32.8 %rows_all.1 = (bf16[2048,1024]{1,0:T(8,128)(2,1)}, bf16[2048,1024]{1,0:T(8,128)(2,1)}, bf16[2048,1024]{1,0:T(8,128)(2,1)}, bf16[2048,1024]{1,0:T(8,128)(2,1)}, f32[8,1024]{1,0:T(8,128)}) custom-call(bf16[2048,1024]{1,0:T(8,128)(2,1)} %get-tuple-element.33.x_ref, bf16[2048,1024]{1,0:T(8,128)(2,1)} %get-tuple-element.39.h2_ref, ...), custom_call_target="tpu_custom_call" | custom-call | flops 20000000000 | bytes 30000000 | tf_op jit(solution)/shard_map/rows_all/pallas_call | solution.py:479
  191.0 0.0 copy-done.7
  191.0 1.4 add.102.small
  192.3 24.8 %weights_all.1.blocks = bf16[192,128,128]{2,1,0:T(8,128)(2,1)} custom-call(bf16[2048,1024]{1,0:T(8,128)(2,1)} %get-tuple-element.37.h1_ref, bf16[2048,256]{1,0:T(8,128)(2,1)} %get-tuple-element.38.ctx_ref, bf16[2048,1024]{1,0:T(8,128)(2,1)} %get-tuple-element.39.h2_ref, bf16[2048,1024]{1,0:T(8,128)(2,1)} %get-tuple-element.44.act_ref, ...), custom_call_target="tpu_custom_call" | custom-call | flops 12999999488 | bytes 30000000 | tf_op jit(solution)/shard_map/weights_all/pallas_call | solution.py:525
  217.2 0.8 fusion.18
  218.0 0.7 select_reduce_fusion.order
  218.6 0.0 copy-start.9
  218.6 0.0 copy-start.10
  218.6 0.0 copy-start.8
  218.6 0.0 copy-start.2
  218.6 79.5 %sums_all.1 = (f32[24,128,128]{2,1,0:T(8,128)}, f32[512,1024]{1,0:T(8,128)}, f32[512,1024]{1,0:T(8,128)}, f32[8,1024]{1,0:T(8,128)}) custom-call(s32[192]{0:T(256)} %select_reduce_fusion.order, bf16[192,128,128]{2,1,0:T(8,128)(2,1)} %weights_all.1.blocks, bf16[2048,1024]{1,0:T(8,128)(2,1)} %get-tuple-element.46.br, bf16[2048,1024]{1,0:T(8,128)(2,1)} %get-tuple-element.47.e, ...), custom_call_target="tpu_custom_call" | custom-call | bytes 30000000 | tf_op jit(solution)/shard_map/sums_all/pallas_call | solution.py:746
  298.1 0.0 copy-start.3
  298.2 0.9 broadcast_multiply_fusion
  299.1 0.0 copy-done.9
  299.1 0.6 rsqrt_multiply_fusion.1
  299.7 0.0 copy-done.10
  299.7 0.6 rsqrt_multiply_fusion.2
  300.3 0.0 copy-done.8
  300.3 0.6 rsqrt_multiply_fusion
  301.0 0.0 copy-done.2
  301.0 0.2 convert_reduce_fusion
  301.2 0.0 copy-start.13
  301.2 0.0 copy-start.12
  301.2 0.4 fusion.8
  301.6 0.0 copy-done.3
  301.7 0.7 fusion.19
  302.4 0.0 copy-done.13
  302.4 0.1 fusion.12
  302.5 0.0 copy-done.12
  302.5 0.0 copy-start.1
  302.5 4.3 %fusion.7 = (f32[512,1024]{1,0:T(8,128)}, bf16[512,1024]{1,0:T(8,128)(2,1)}) fusion(bf16[512,1024]{1,0:T(8,128)(2,1)S(1)} %copy-done.2, f32[512,1024]{1,0:T(8,128)} %get-tuple-element.51, bf16[512,1024]{1,0:T(8,128)(2,1)} %dy.1, f32[512]{0:T(512)S(1)} %get-tuple-element.71, f32[512]{0:T(512)S(1)} %get-tuple-element.72, f32[512]{0:T(512)S(1)} %add_rsqrt_fusion, ...), kind=kLoop, calls=%fused_computation.10 | loop fusion | flops 7340032 | bytes 9455616 | tf_op jit(solution)/shard_map/add | solution.py:815
  306.9 0.0 copy-done
  306.9 0.0 copy-done.1
  306.9 0.0 copy-start.4
  306.9 1.6 fusion.21
  308.5 0.0 copy-done.4
  308.5 0.0 copy-start.5
  308.5 2.9 convolution_multiply_fusion
  311.4 0.0 copy-done.5
  311.4 0.0 copy-start.6
  311.4 4.0 %add_multiply_fusion = f32[24,128,128]{2,1,0:T(8,128)} fusion(f32[24,128,128]{2,1,0:T(8,128)S(1)} %copy-done.5, f32[24,128,128]{2,1,0:T(8,128)S(1)} %copy-done.1), kind=kOutput, calls=%fused_computation.15 | convolution fusion | flops 604766208 | bytes 4718592 | tf_op jit(solution)/shard_map/sji,sjk->sik/dot_general | solution.py:824
  315.3 0.0 copy-done.6
  315.3 4.6 %add_multiply_fusion.1 = f32[24,128,128]{2,1,0:T(8,128)} fusion(f32[24,128,128]{2,1,0:T(8,128)S(1)} %copy-done.6, f32[24,128,128]{2,1,0:T(8,128)S(1)} %copy-done.1), kind=kOutput, calls=%fused_computation.16 | convolution fusion | flops 604766208 | bytes 4718592 | tf_op jit(solution)/shard_map/sij,skj->sik/dot_general | solution.py:821
  319.9 1.1 copy.40
  (8 shorter events, 0.1 us)
Async XLA Ops:
  0.6 306.2 %copy-start = (f32[24,128,128]{2,1,0:T(8,128)S(1)}, f32[24,128,128]{2,1,0:T(8,128)}, u32[]{:S(2)}) copy-start(f32[24,128,128]{2,1,0:T(8,128)} %param.34) | copy-start | bytes 4718596
  0.7 96.4 %copy-start.11 = (f32[768]{0:T(1024)S(1)}, f32[768]{0:T(1024)}, u32[]{:S(2)}) copy-start(f32[768]{0:T(1024)} %param.26) | copy-start | bytes 9220
  158.2 32.8 %copy-start.7 = (f32[8,1024]{1,0:T(8,128)S(1)}, f32[8,1024]{1,0:T(8,128)}, u32[]{:S(2)}) copy-start(f32[8,1024]{1,0:T(8,128)} %get-tuple-element.48) | copy-start | bytes 98308
  218.6 80.5 %copy-start.9 = (f32[1024]{0:T(1024)S(1)}, f32[1024]{0:T(1024)}, u32[]{:S(2)}) copy-start(f32[1024]{0:T(1024)} %param.38) | copy-start | bytes 12292
  218.6 81.1 %copy-start.10 = (f32[768]{0:T(1024)S(1)}, f32[768]{0:T(1024)}, u32[]{:S(2)}) copy-start(f32[768]{0:T(1024)} %param.37) | copy-start | bytes 9220
  218.6 81.7 %copy-start.8 = (f32[6,1024]{1,0:T(8,128)S(1)}, f32[6,1024]{1,0:T(8,128)}, u32[]{:S(2)}) copy-start(f32[6,1024]{1,0:T(8,128)} %param.36) | copy-start | bytes 73732
  218.6 82.3 %copy-start.2 = (bf16[512,1024]{1,0:T(8,128)(2,1)S(1)}, bf16[512,1024]{1,0:T(8,128)(2,1)}, u32[]{:S(2)}) copy-start(bf16[512,1024]{1,0:T(8,128)(2,1)} %x.1) | copy-start | bytes 3145732
  298.1 3.5 %copy-start.3 = (f32[512,1024]{1,0:T(8,128)S(1)}, f32[512,1024]{1,0:T(8,128)}, u32[]{:S(2)}) copy-start(f32[512,1024]{1,0:T(8,128)} %get-tuple-element.51) | copy-start | bytes 6291460
  301.2 1.2 copy-start.13
  301.2 1.3 copy-start.12
  302.5 4.3 %copy-start.1 = (f32[24,128,128]{2,1,0:T(8,128)S(1)}, f32[24,128,128]{2,1,0:T(8,128)}, u32[]{:S(2)}) copy-start(f32[24,128,128]{2,1,0:T(8,128)} %get-tuple-element.87) | copy-start | bytes 4718596
  306.9 1.6 copy-start.4
  308.5 2.9 copy-start.5
  311.4 4.0 %copy-start.6 = (f32[24,128,128]{2,1,0:T(8,128)S(1)}, f32[24,128,128]{2,1,0:T(8,128)}, u32[]{:S(2)}) copy-start(f32[24,128,128]{2,1,0:T(8,128)} %param.32) | copy-start | bytes 4718596

commit v2 on v1

--- a/solution.py
+++ b/solution.py
@@ -31,16 +31,11 @@
     return (accum_next, -adagrad_rate * grad_vec * lax.rsqrt(accum_next))
 
 
-def rotary_wide():
+def rotary_rows():
     half = ROT // 2
     inverse = np.power(np.float32(10000.0), -(np.arange(half, dtype=np.float32) * np.float32(2.0 / ROT)))
-    angles = np.arange(LEN, dtype=np.float32)[:, None] * inverse.astype(np.float32)[None, :]
-    cosine, sine = np.cos(angles), np.sin(angles)
-    rest = HEAD - ROT
-    cos_one = np.concatenate([cosine, cosine, np.ones((LEN, rest), np.float32)], axis=1)
-    sin_one = np.concatenate([-sine, sine, np.zeros((LEN, rest), np.float32)], axis=1)
-    wide = np.concatenate([cos_one, cos_one, sin_one, sin_one], axis=1)
-    return wide.astype(np.float32)
+    angles = inverse.astype(np.float32)[:, None] * np.arange(LEN, dtype=np.float32)[None, :]
+    return np.concatenate([np.cos(angles), np.sin(angles)], axis=0).astype(np.float32)
 
 
 def ring_place(me, count):
@@ -225,69 +220,6 @@
     pl.semaphore_wait(barrier, len(devices))
 
 
-def gather_kernel(count, x, dy, wq, wd, w1, w2, xf, dyf, wqf, wdf, w1f, w2f, rs, rr, ro, gs, gr, go):
-    ring = Ring(count)
-    locals_, fulls = (wq, wd, w1, w2), (wqf, wdf, w1f, w2f)
-    gather = Gather(ring, locals_, fulls, gs, gr)
-    rx = Rows(x, xf, rs.at[0], rr.at[0], ro.at[0])
-    ry = Rows(dy, dyf, rs.at[1], rr.at[1], ro.at[1])
-    greet([ring.peer[0], ring.peer[1], (ring.me, rx.near), (ring.me, rx.across)])
-    gather.begin(0)
-    rx.begin_cross()
-    rx.begin_near()
-    ry.begin_near()
-    own = []
-    for w in range(4):
-        rows = locals_[w].shape[0]
-        own.append(
-            pltpu.make_async_copy(
-                locals_[w], fulls[w].at[pl.ds(pl.multiple_of(ring.me * rows, 16), rows)], go.at[w]
-            )
-        )
-        own[-1].start()
-    far = count // 2
-    for w in range(4):
-        for_hops(1, far, lambda hop: gather.forward(w, hop, False), count)
-        if w < 3:
-            gather.begin(w + 1)
-        gather.forward(w, far, True)
-        if w == 1:
-            rx.pass_on()
-            ry.begin_cross()
-    ry.pass_on()
-    for w in range(4):
-        gather.finish(w)
-        own[w].wait()
-    rx.finish()
-    ry.finish()
-
-
-def gather_all(count, x, dy, wq, wd, w1, w2):
-    far = count // 2
-    outs = [jax.ShapeDtypeStruct((4 * v.shape[0], v.shape[1]), v.dtype) for v in (x, dy)]
-    outs += [jax.ShapeDtypeStruct((count * v.shape[0], v.shape[1]), v.dtype) for v in (wq, wd, w1, w2)]
-    moved = sum(v.size * 2 for v in outs)
-    return pl.pallas_call(
-        functools.partial(gather_kernel, count),
-        out_shape=outs,
-        in_specs=[pl.BlockSpec(memory_space=pl.ANY)] * 6,
-        out_specs=[pl.BlockSpec(memory_space=pl.ANY)] * 6,
-        scratch_shapes=[
-            pltpu.SemaphoreType.DMA((2, 5)),
-            pltpu.SemaphoreType.DMA((2, 5)),
-            pltpu.SemaphoreType.DMA((2,)),
-            pltpu.SemaphoreType.DMA((16 * far,)),
-            pltpu.SemaphoreType.DMA((16 * far,)),
-            pltpu.SemaphoreType.DMA((4,)),
-        ],
-        compiler_params=pltpu.CompilerParams(
-            collective_id=0, has_side_effects=True, vmem_limit_bytes=VMEM_LIMIT
-        ),
-        cost_estimate=pl.CostEstimate(flops=0, bytes_accessed=moved, transcendentals=0),
-        name="gather_all",
-    )(x, dy, wq, wd, w1, w2)
-
-
 def dot_nn(a, b):
     return lax.dot_general(a, b, (((1,), (0,)), ((), ())), preferred_element_type=f32)
 
@@ -308,124 +240,330 @@
     return centered * scale, scale
 
 
-def swap_halves(v):
-    half = ROT // 2
-    lane = lax.broadcasted_iota(jnp.int32, v.shape, 1) % HEAD
-    return jnp.where(lane < half, pltpu.roll(v, v.shape[1] - half, 1), pltpu.roll(v, half, 1))
-
-
-def attention_kernel(
-    heads, lim_ref, x_ref, dy_ref, wq_ref, wd_ref, gain_ref, bias_ref, qb_ref, rot_ref,
-    h1_ref, h2_ref, dyb_ref, ctx_ref, dproj_ref, sum_ref,
-    qs, ks, vs, dcs, dqs, dks, dvs, ctxs,
+def mixed_kernel(
+    count, lim_ref, gain_ref, bias_ref, qb_ref, rot_ref, x, dy, wqd, w1, w2,
+    x_out, h1_out, dyb_out, ctx_out, dproj_out, wqd_out, w1f, w2f, sum_ref,
+    xf, dyf, wf, h1s, ctxs, dps, qt, kt, vt, dct, ctt, dqt, kr, vr, dks, dvs,
+    rs, rr, ro, gs, gr, go, os,
 ):
-    seq = pl.program_id(0)
-    limit = lim_ref[seq]
-
-    @pl.when(seq == 0)
-    def _():
-        sum_ref[...] = jnp.zeros_like(sum_ref)
-
-    @pl.loop(0, LEN // TILE)
-    def _(i):
-        rows = pl.ds(pl.multiple_of(i * TILE, TILE), TILE)
-        xhat, _ = normed(x_ref[rows, :].astype(f32))
-        h1 = (xhat * gain_ref[0:1, :] + bias_ref[0:1, :]).astype(bf16)
-        h1_ref[rows, :] = h1
-        h2_ref[rows, :] = (xhat * gain_ref[1:2, :] + bias_ref[1:2, :]).astype(bf16)
-        proj = dot_nn(h1, wq_ref[...]) + qb_ref[...]
+    ring = Ring(count)
+    half_cols = wqd.shape[1] // 2
+    pair_cols = 6 * HEAD
+    views = [(wqd.at[:, pl.ds(p * half_cols, half_cols)], wf.at[:, pl.ds(p * half_cols, half_cols)]) for p in (0, 1)]
+    views += [(w1, w1f), (w2, w2f)]
+    gather = Gather(ring, [v[0] for v in views], [v[1] for v in views], gs, gr)
+    rx = Rows(x, xf, rs.at[0], rr.at[0], ro.at[0])
+    ry = Rows(dy, dyf, rs.at[1], rr.at[1], ro.at[1])
+    greet([ring.peer[0], ring.peer[1], (ring.me, rx.near), (ring.me, rx.across)])
+    far = count // 2
+    own = []
+    for k, (local, full) in enumerate(((wqd, wf), (w1, w1f), (w2, w2f))):
+        rows = local.shape[0]
+        own.append(
+            pltpu.make_async_copy(local, full.at[pl.ds(pl.multiple_of(ring.me * rows, 16), rows)], go.at[k])
+        )
+    rx.begin_near()
+    gather.begin(0)
+    rx.begin_cross()
+    ry.begin_near()
+    for copy in own:
+        copy.start()
+    sum_ref[...] = jnp.zeros_like(sum_ref)
+    tensor = ring.tensor
+    tiles = LEN // TILE
+
+    def whole_ring(w):
+        for_hops(1, far, lambda hop: gather.forward(w, hop, False), count)
+        gather.forward(w, far, True)
+
+    def hop_at(w, hop):
+        if count == 8:
+            gather.forward(w, hop, hop == far)
+        elif hop == 4:
+            whole_ring(w)
+
+    def rows_of(seq, i):
+        return pl.ds(pl.multiple_of(seq * LEN + i * TILE, TILE), TILE)
+
+    def norm_tile(seq, i):
+        rows = rows_of(seq, i)
+        xhat, _ = normed(xf[rows, :].astype(f32))
+        h1s[rows, :] = (xhat * gain_ref[0:1, :] + bias_ref[0:1, :]).astype(bf16)
+
+    def mask_tile(seq, i):
+        rows = rows_of(seq, i)
         place = i * TILE + lax.broadcasted_iota(jnp.int32, (TILE, 1), 0)
-        dy = jnp.where(place < limit, dy_ref[rows, :].astype(f32), 0.0)
-        sum_ref[4:5, :] += jnp.sum(dy, axis=0, keepdims=True)
-        dyb = dy.astype(bf16)
-        dyb_ref[rows, :] = dyb
-        dctx = dot_nn(dyb, wd_ref[...]).astype(bf16)
-        cosine, sine = rot_ref[rows, 0:128], rot_ref[rows, 128:256]
-        for h in range(heads):
-            pair = proj[:, 3 * HEAD * h : 3 * HEAD * h + 2 * HEAD]
-            pair = pair * cosine + swap_halves(pair) * sine
-            qs[h, rows, :] = (pair[:, :HEAD].astype(bf16) * 0.125).astype(bf16)
-            ks[h, rows, :] = pair[:, HEAD:].astype(bf16)
-            vs[h, rows, :] = proj[:, 3 * HEAD * h + 2 * HEAD : 3 * HEAD * (h + 1)].astype(bf16)
-            dcs[h, rows, :] = dctx[:, HEAD * h : HEAD * (h + 1)]
-
-    @pl.loop(0, heads)
-    def _(h):
-        for i in reversed(range(LEN // TILE)):
-            seen = (i + 1) * TILE
-            rows = slice(i * TILE, seen)
-            q, do = qs[h, rows, :], dcs[h, rows, :]
-            k, v = ks[h, :seen, :], vs[h, :seen, :]
-            s = dot_nt(q, k)
-            col = lax.broadcasted_iota(jnp.int32, (TILE, seen), 1)
-            row = lax.broadcasted_iota(jnp.int32, (TILE, seen), 0) + i * TILE
-            s = jnp.where((col <= row) & (col < limit), s, masked_score)
-            p = jnp.exp(s - jnp.max(s, axis=1, keepdims=True))
-            p = p * (1.0 / jnp.sum(p, axis=1, keepdims=True))
-            pb = p.astype(bf16)
-            ctxs[h, rows, :] = dot_nn(pb, v).astype(bf16)
-            dp = dot_nt(do, v)
-            ds = (p * (dp - jnp.sum(p * dp, axis=1, keepdims=True))).astype(bf16)
-            dqs[h, rows, :] = dot_nn(ds, k) * 0.125
-            dv_part = dot_tn(pb, do)
-            dk_part = dot_tn(ds, q)
-            if i == LEN // TILE - 1:
-                dvs[h, :, :] = dv_part
-                dks[h, :, :] = dk_part
+        kept = jnp.where(place < lim_ref[seq], dyf[rows, :].astype(f32), 0.0)
+        sum_ref[4:5, :] += jnp.sum(kept, axis=0, keepdims=True)
+        dyf[rows, :] = kept.astype(bf16)
+
+    def turned(first, second, cosine, sine):
+        return first * cosine - second * sine, second * cosine + first * sine
+
+    def prepare_tile(seq, pair, i):
+        rows = rows_of(seq, i)
+        cols = pl.ds(pl.multiple_of(i * TILE, TILE), TILE)
+        begin = pl.multiple_of(pair * half_cols, BLOCK)
+        proj = dot_nn(h1s[rows, :], wf[:, pl.ds(begin, pair_cols)])
+        proj = proj + qb_ref[:, pl.ds(pl.multiple_of(pair * pair_cols, BLOCK), pair_cols)]
+        proj = proj.T
+        dctx = dot_nn(dyf[rows, :], wf[:, pl.ds(begin + pair_cols, 2 * HEAD)]).T
+        cosine, sine = rot_ref[0:8, cols], rot_ref[8:16, cols]
+        key = i * TILE + lax.broadcasted_iota(jnp.int32, (16, TILE), 1)
+        row = lax.broadcasted_iota(jnp.int32, (16, TILE), 0)
+        ones = jnp.where(row == 0, 1.0, 0.0)
+        hidden = jnp.where((row == 0) & (key >= lim_ref[seq]), masked_score, 0.0)
+        for hh in range(2):
+            base = 3 * HEAD * hh
+            q0, q1 = turned(proj[base : base + 8], proj[base + 8 : base + 16], cosine, sine)
+            q = jnp.concatenate([q0, q1, proj[base + 16 : base + HEAD]], axis=0)
+            q = q.astype(bf16).astype(f32) * 0.125
+            qt[hh, :, cols] = jnp.concatenate([q, ones], axis=0).astype(bf16)
+            base += HEAD
+            k0, k1 = turned(proj[base : base + 8], proj[base + 8 : base + 16], cosine, sine)
+            k = jnp.concatenate([k0, k1, proj[base + 16 : base + HEAD]], axis=0)
+            kt[hh, :, cols] = k.astype(bf16)
+            kr[hh, cols, :] = jnp.concatenate([k, hidden], axis=0).T.astype(bf16)
+            base += HEAD
+            v = proj[base : base + HEAD]
+            vt[hh, :, cols] = jnp.concatenate([v, ones], axis=0).astype(bf16)
+            vr[hh, cols, :] = v.T.astype(bf16)
+            dct[hh, :, cols] = dctx[HEAD * hh : HEAD * (hh + 1)].astype(bf16)
+
+    def attend(hh, i):
+        here = slice(i * TILE, (i + 1) * TILE)
+        chunks = [slice(c * TILE, (c + 1) * TILE) for c in range(i + 1)]
+        q = qt[hh, :, here]
+        scores = [dot_nn(kr[hh, c, :], q) for c in chunks]
+        key = lax.broadcasted_iota(jnp.int32, (TILE, TILE), 0)
+        query = lax.broadcasted_iota(jnp.int32, (TILE, TILE), 1)
+        scores[i] = jnp.where(key <= query, scores[i], masked_score)
+        top = jnp.max(scores[0], axis=0, keepdims=True)
+        for s in scores[1:]:
+            top = jnp.maximum(top, jnp.max(s, axis=0, keepdims=True))
+        probs = [jnp.exp(s - top).astype(bf16) for s in scores]
+        total = dot_nn(vt[hh, :, chunks[0]], probs[0])
+        for c, p in zip(chunks[1:], probs[1:]):
+            total = total + dot_nn(vt[hh, :, c], p)
+        inverse = 1.0 / total[HEAD : HEAD + 1]
+        context = total[:HEAD] * inverse
+        ctt[hh, :, here] = context
+        grad = dct[hh, :, here].astype(f32)
+        delta = jnp.sum(grad * context, axis=0, keepdims=True) * inverse
+        grad = (grad * inverse).astype(bf16)
+        dq = None
+        for n, (c, p) in enumerate(zip(chunks, probs)):
+            dp = dot_nn(vr[hh, c, :], grad)
+            ds = (p.astype(f32) * (dp - delta)).astype(bf16)
+            part = dot_nn(kt[hh, :, c], ds)
+            dq = part if dq is None else dq + part
+            dk = dot_nt(ds, q[:HEAD])
+            dv = dot_nt(p, grad)
+            if i == tiles - 1:
+                dks[hh, c, :] = dk
+                dvs[hh, c, :] = dv
             else:
-                dvs[h, :seen, :] += dv_part
-                dks[h, :seen, :] += dk_part
-
-    @pl.loop(0, LEN // TILE)
-    def _(i):
-        rows = pl.ds(pl.multiple_of(i * TILE, TILE), TILE)
-        cosine, sine = rot_ref[rows, 0:128], rot_ref[rows, 128:256]
-        for h in range(heads):
-            pair = jnp.concatenate([dqs[h, rows, :], dks[h, rows, :]], axis=1)
-            pair = (pair * cosine - swap_halves(pair) * sine).astype(bf16)
-            low = dvs[h, rows, :].astype(bf16)
-            lo = 3 * HEAD * h
-            dproj_ref[rows, lo : lo + 2 * HEAD] = pair
-            dproj_ref[rows, lo + 2 * HEAD : lo + 3 * HEAD] = low
-            sum_ref[5:6, lo : lo + 2 * HEAD] += jnp.sum(pair.astype(f32), axis=0, keepdims=True)
-            sum_ref[5:6, lo + 2 * HEAD : lo + 3 * HEAD] += jnp.sum(low.astype(f32), axis=0, keepdims=True)
-            ctx_ref[rows, HEAD * h : HEAD * (h + 1)] = ctxs[h, rows, :]
-
-
-def attention_all(limits, xf, dyf, wqf, wdf, gains, biases, qkv_bias, rot):
-    seqs = limits.shape[0]
-    width = xf.shape[1]
-    heads = wqf.shape[1] // (3 * HEAD)
-
-    def per_seq(cols):
-        return pl.BlockSpec((LEN, cols), lambda s: (s, 0))
-
-    def whole(shape):
-        return pl.BlockSpec(shape, lambda s: (0, 0))
-
-    out = lambda cols: jax.ShapeDtypeStruct((seqs * LEN, cols), bf16)
-    per_head = lambda dtype: pltpu.VMEM((heads, LEN, HEAD), dtype)
+                dks[hh, c, :] += dk
+                dvs[hh, c, :] += dv
+        dqt[hh, :, here] = dq * 0.125
+
+    def collect_tile(seq, pair, i):
+        rows = rows_of(seq, i)
+        cols = pl.ds(pl.multiple_of(i * TILE, TILE), TILE)
+        cosine, sine = rot_ref[0:8, cols], rot_ref[8:16, cols]
+        pieces = []
+        for hh in range(2):
+            for grad in (dqt[hh, :, cols], dks[hh, cols, :].T):
+                pieces += [*turned(grad[0:8], grad[8:16], cosine, -sine), grad[16:HEAD]]
+            pieces.append(dvs[hh, cols, :].T)
+        low = jnp.concatenate(pieces, axis=0).T.astype(bf16)
+        wide = pl.ds(pl.multiple_of(pair * pair_cols, BLOCK), pair_cols)
+        dps[rows, wide] = low
+        sum_ref[5:6, wide] += jnp.sum(low.astype(f32), axis=0, keepdims=True)
+        ctx = jnp.concatenate([ctt[0, :, cols], ctt[1, :, cols]], axis=0).T
+        ctxs[rows, pl.ds(pl.multiple_of(pair * 2 * HEAD, BLOCK), 2 * HEAD)] = ctx.astype(bf16)
+
+    def save(k, src, dst, seq):
+        rows = pl.ds(pl.multiple_of(seq * LEN, LEN), LEN)
+        return pltpu.make_async_copy(src.at[rows], dst.at[rows], os.at[k])
+
+    first = tensor // 2
+
+    @pl.loop(0, 4)
+    def _(g):
+        turn, pair = g // 2, g % 2
+        seq = turn + (1 - 2 * turn) * first
+
+        def at(place):
+            return pl.when(g == place)
+
+        @at(0)
+        def _():
+            rx.keep().wait()
+            rx.pair().wait_recv()
+
+        @at(2)
+        def _():
+            for piece in range(2):
+                rx.onward(piece).wait_recv()
+
+        @pl.when(pair == 0)
+        def _():
+            @pl.loop(0, tiles)
+            def _(i):
+                norm_tile(seq, i)
+
+                @pl.when((g == 0) & (i == 0))
+                def _():
+                    hop_at(0, 1)
+                    gather.begin(1)
+
+                @pl.when((g == 0) & (i == 1))
+                def _():
+                    hop_at(0, 2)
+                    hop_at(1, 1)
+
+                @pl.when((g == 0) & (i == 2))
+                def _():
+                    hop_at(0, 3)
+                    hop_at(1, 2)
+                    gather.begin(2)
+
+            save(0, xf, x_out, seq).start()
+            save(1, h1s, h1_out, seq).start()
+
+        @at(0)
+        def _():
+            hop_at(0, 4)
+            own[0].wait()
+            ry.keep().wait()
+            ry.pair().wait_recv()
+
+        @at(1)
+        def _():
+            hop_at(2, 1)
+
+        @at(2)
+        def _():
+            ry.pass_on()
+            for piece in range(2):
+                ry.onward(piece).wait()
+
+        @at(3)
+        def _():
+            hop_at(3, 3)
+
+        @pl.when(pair == 0)
+        def _():
+            @pl.loop(0, tiles)
+            def _(i):
+                mask_tile(seq, i)
+
+            save(2, dyf, dyb_out, seq).start()
+
+        @pl.loop(0, tiles)
+        def _(i):
+            prepare_tile(seq, pair, i)
+
+        @at(0)
+        def _():
+            hop_at(1, 3)
+            gather.begin(3)
+
+        @at(1)
+        def _():
+            hop_at(3, 1)
+
+        @pl.loop(0, 2)
+        def _(hh):
+            for i in reversed(range(tiles)):
+                attend(hh, i)
+
+            @pl.when((g == 0) & (hh == 0))
+            def _():
+                hop_at(1, 4)
+                rx.pass_on()
+                ry.begin_cross()
+
+            @pl.when((g == 1) & (hh == 0))
+            def _():
+                hop_at(2, 2)
+
+            @pl.when((g == 1) & (hh == 1))
+            def _():
+                hop_at(3, 2)
+
+            @pl.when((g == 2) & (hh == 0))
+            def _():
+                hop_at(2, 3)
+
+            @pl.when((g == 3) & (hh == 0))
+            def _():
+                hop_at(2, 4)
+
+        @pl.loop(0, tiles)
+        def _(i):
+            collect_tile(seq, pair, i)
+
+        @pl.when(pair == 1)
+        def _():
+            save(3, ctxs, ctx_out, seq).start()
+            save(4, dps, dproj_out, seq).start()
+
+        @pl.when(pair == 1)
+        def _():
+            for k, (src, dst) in enumerate(
+                ((xf, x_out), (h1s, h1_out), (dyf, dyb_out), (ctxs, ctx_out), (dps, dproj_out))
+            ):
+                save(k, src, dst, seq).wait()
+
+    keep = pltpu.make_async_copy(wf, wqd_out, os.at[5])
+    keep.start()
+    hop_at(3, 4)
+    for w in range(4):
+        gather.finish(w)
+    own[1].wait()
+    own[2].wait()
+    rx.pair().wait_send()
+    ry.pair().wait_send()
+    for piece in range(2):
+        rx.cross(piece).wait_send()
+        rx.onward(piece).wait_send()
+        ry.cross(piece).wait_send()
+    keep.wait()
+
+
+def mixed_all(count, limits, gains, biases, qkv_bias, rot, x, dy, wqd, w1, w2):
+    far = count // 2
+    rows, width = 4 * x.shape[0], x.shape[1]
+    ctx_cols, proj_cols = 4 * HEAD, qkv_bias.shape[1]
+    out = lambda r, c: jax.ShapeDtypeStruct((r, c), bf16)
+    full = lambda v: out(count * v.shape[0], v.shape[1])
+    any_, vmem = pl.BlockSpec(memory_space=pl.ANY), pl.BlockSpec(memory_space=pltpu.VMEM)
+    dma = lambda *n: pltpu.SemaphoreType.DMA(n)
+    buf = lambda dtype, *shape: pltpu.VMEM(shape, dtype)
     return pl.pallas_call(
-        functools.partial(attention_kernel, heads),
-        grid=(seqs,),
+        functools.partial(mixed_kernel, count),
         out_shape=[
-            out(width), out(width), out(width), out(heads * HEAD), out(heads * 3 * HEAD),
-            jax.ShapeDtypeStruct((8, width), f32),
+            out(rows, width), out(rows, width), out(rows, width), out(rows, ctx_cols), out(rows, proj_cols),
+            full(wqd), full(w1), full(w2), jax.ShapeDtypeStruct((8, width), f32),
         ],
-        in_specs=[
-            pl.BlockSpec(memory_space=pltpu.SMEM),
-            per_seq(width), per_seq(width), whole(wqf.shape), whole(wdf.shape), whole(gains.shape),
-            whole(biases.shape), whole(qkv_bias.shape), whole(rot.shape),
+        in_specs=[pl.BlockSpec(memory_space=pltpu.SMEM)] + [vmem] * 4 + [any_] * 5,
+        out_specs=[any_] * 8 + [vmem],
+        scratch_shapes=[
+            buf(bf16, rows, width), buf(bf16, rows, width), buf(bf16, width, wqd.shape[1]),
+            buf(bf16, rows, width), buf(bf16, rows, ctx_cols), buf(bf16, rows, proj_cols),
+            buf(bf16, 2, HEAD + 16, LEN), buf(bf16, 2, HEAD, LEN), buf(bf16, 2, HEAD + 16, LEN),
+            buf(bf16, 2, HEAD, LEN), buf(f32, 2, HEAD, LEN), buf(f32, 2, HEAD, LEN),
+            buf(bf16, 2, LEN, HEAD + 16), buf(bf16, 2, LEN, HEAD), buf(f32, 2, LEN, HEAD), buf(f32, 2, LEN, HEAD),
+            dma(2, 5), dma(2, 5), dma(2), dma(16 * far), dma(16 * far), dma(3), dma(6),
         ],
-        out_specs=[
-            per_seq(width), per_seq(width), per_seq(width), per_seq(heads * HEAD),
-            per_seq(heads * 3 * HEAD), whole((8, width)),
-        ],
-        scratch_shapes=[per_head(bf16)] * 4 + [per_head(f32)] * 3 + [per_head(bf16)],
-        compiler_params=pltpu.CompilerParams(vmem_limit_bytes=VMEM_LIMIT),
-        cost_estimate=pl.CostEstimate(flops=int(1e10), bytes_accessed=int(3e7), transcendentals=int(1e7)),
-        name="attention_all",
-    )(limits, xf, dyf, wqf, wdf, gains, biases, qkv_bias, rot)
+        compiler_params=pltpu.CompilerParams(
+            collective_id=0, has_side_effects=True, vmem_limit_bytes=VMEM_LIMIT
+        ),
+        cost_estimate=pl.CostEstimate(flops=int(2e10), bytes_accessed=int(4e7), transcendentals=int(1e7)),
+        name="mixed_all",
+    )(limits, gains, biases, qkv_bias, rot, x, dy, wqd, w1, w2)
 
 
 def gelu_both(x):
@@ -439,23 +577,32 @@
 
 
 def rows_kernel(
-    x_ref, h2_ref, dyb_ref, ctx_ref, dproj_ref, wq_ref, wd_ref, w1_ref, w2_ref, gain_ref, fb_ref,
-    act_ref, dab_ref, br_ref, e_ref, sum_ref,
+    x_ref, dyb_ref, ctx_ref, dproj_ref, wqd_ref, w1_ref, w2_ref, gain_ref, bias_ref, fb_ref,
+    h2_ref, act_ref, dab_ref, br_ref, e_ref, sum_ref,
 ):
     @pl.when(pl.program_id(0) == 0)
     def _():
         sum_ref[...] = jnp.zeros_like(sum_ref)
 
-    pre = dot_nn(h2_ref[...], w1_ref[...]) + fb_ref[...]
+    xhat, _ = normed(x_ref[...].astype(f32))
+    h2 = (xhat * gain_ref[1:2, :] + bias_ref[1:2, :]).astype(bf16)
+    h2_ref[...] = h2
+    pre = dot_nn(h2, w1_ref[...]) + fb_ref[...]
     act, slope = gelu_both(pre)
     act = act.astype(bf16)
     act_ref[...] = act
     dab = (dot_nn(dyb_ref[...], w2_ref[...]) * slope).astype(bf16)
     dab_ref[...] = dab
-    br_ref[...] = (dot_nt(ctx_ref[...], wd_ref[...]) + dot_nt(act, w2_ref[...])).astype(bf16)
+    br = dot_nt(act, w2_ref[...])
     dh2 = dot_nt(dab, w1_ref[...])
-    dh1 = dot_nt(dproj_ref[...], wq_ref[...])
-    xhat, _ = normed(x_ref[...].astype(f32))
+    dh1 = None
+    wide, thin = 6 * HEAD, 2 * HEAD
+    for p in range(2):
+        lo = p * (wide + thin)
+        br = br + dot_nt(ctx_ref[:, p * thin : (p + 1) * thin], wqd_ref[:, lo + wide : lo + wide + thin])
+        part = dot_nt(dproj_ref[:, p * wide : (p + 1) * wide], wqd_ref[:, lo : lo + wide])
+        dh1 = part if dh1 is None else dh1 + part
+    br_ref[...] = br.astype(bf16)
     e_ref[...] = (dh1 * gain_ref[0:1, :] + dh2 * gain_ref[1:2, :]).astype(bf16)
     total = lambda v: jnp.sum(v, axis=0, keepdims=True)
     sum_ref[0:1, :] += total(dh1 * xhat)
@@ -465,7 +612,7 @@
     sum_ref[6:7, :] += total(dab.astype(f32))
 
 
-def rows_all(xf, h2, dyb, ctx, dproj, wqf, wdf, w1f, w2f, gains, fc1_bias):
+def rows_all(xf, dyb, ctx, dproj, wqdf, w1f, w2f, gains, biases, fc1_bias):
     rows, width = xf.shape
 
     def tile(cols):
@@ -479,14 +626,16 @@
     return pl.pallas_call(
         rows_kernel,
         grid=(rows // TILE,),
-        out_shape=[out(hidden), out(hidden), out(width), out(width), jax.ShapeDtypeStruct((8, width), f32)],
-        in_specs=[tile(v.shape[1]) for v in (xf, h2, dyb, ctx, dproj)]
-        + [whole(v) for v in (wqf, wdf, w1f, w2f, gains, fc1_bias)],
-        out_specs=[tile(hidden), tile(hidden), tile(width), tile(width), pl.BlockSpec((8, width), lambda s: (0, 0))],
+        out_shape=[out(width), out(hidden), out(hidden), out(width), out(width)]
+        + [jax.ShapeDtypeStruct((8, width), f32)],
+        in_specs=[tile(v.shape[1]) for v in (xf, dyb, ctx, dproj)]
+        + [whole(v) for v in (wqdf, w1f, w2f, gains, biases, fc1_bias)],
+        out_specs=[tile(width), tile(hidden), tile(hidden), tile(width), tile(width)]
+        + [pl.BlockSpec((8, width), lambda s: (0, 0))],
         compiler_params=pltpu.CompilerParams(vmem_limit_bytes=VMEM_LIMIT),
         cost_estimate=pl.CostEstimate(flops=int(2e10), bytes_accessed=int(3e7), transcendentals=int(4e6)),
         name="rows_all",
-    )(xf, h2, dyb, ctx, dproj, wqf, wdf, w1f, w2f, gains, fc1_bias)
+    )(xf, dyb, ctx, dproj, wqdf, w1f, w2f, gains, biases, fc1_bias)
 
 
 def weights_kernel(plan, h1_ref, ctx_ref, h2_ref, act_ref, dproj_ref, dyb_ref, dab_ref, g_ref):
@@ -792,14 +941,17 @@
     places = jnp.arange(blocks_tensor, dtype=jnp.int32)
     order = jnp.sum(jnp.where(position[:, None] == places[None, :], places[:, None], 0), axis=0)
 
-    xf, dyf, wqf, wdf, w1f, w2f = gather_all(
-        dp_count, tokens, out_grad, qkv_weight, dense_weight.T, fc1_weight, fc2_weight.T
+    wide, thin = 6 * HEAD, 2 * HEAD
+    dense_turned = dense_weight.T
+    wqd = jnp.concatenate(
+        [qkv_weight[:, :wide], dense_turned[:, :thin], qkv_weight[:, wide:], dense_turned[:, thin:]], axis=1
     )
-    h1, h2, dyb, ctx, dproj, sum_a = attention_all(
-        seq_lengths, xf, dyf, wqf, wdf, norm_gains, row_biases, qkv_bias[None], jnp.asarray(rotary_wide())
+    xf, h1, dyb, ctx, dproj, wqdf, w1f, w2f, sum_a = mixed_all(
+        dp_count, seq_lengths, norm_gains, row_biases, qkv_bias[None], jnp.asarray(rotary_rows()),
+        tokens, out_grad, wqd, fc1_weight, fc2_weight.T,
     )
-    act, dab, br, e, sum_b = rows_all(
-        xf, h2, dyb, ctx, dproj, wqf, wdf, w1f, w2f, norm_gains, fc1_bias[None]
+    h2, act, dab, br, e, sum_b = rows_all(
+        xf, dyb, ctx, dproj, wqdf, w1f, w2f, norm_gains, row_biases, fc1_bias[None]
     )
     blocks = weights_all(h1, ctx, h2, act, dproj, dyb, dab)
     own_grad, branch, e_sum, small = sums_all(dp_count, grad_scale, order, blocks, br, e, sum_a + sum_b)

time: 321 us -> 264 us (0.82)
  Pallas kernels: 291 us -> 232 us
    pallas_call x3 -> x2, Pallas kernels: 186 us -> 128 us  [the longest x1 92.2 us: mixed_all(): pl.pallas_call(functools.partial(mixed_kernel, count), out_shape=[out(row...]
where the time goes in v2:
time: 264 us
  Pallas kernels  232 us (88%)
  matrix products  13 us (5%)
  other arithmetic  11.4 us (4%)
  local copies, waits for them, and re-layouts  6.3 us (2%)
    pallas_call x1, Pallas kernels, mixed_all(): pl.pallas_call(functools.partial(mixed_kernel, count), out_shape=[out(row...  92.2 us
    pallas_call x1, Pallas kernels, sums_all(): pl.pallas_call(functools.partial(sums_kernel, count, scale), out_shape=[j...  79.5 us
    pallas_call x1, Pallas kernels, rows_all(): pl.pallas_call(rows_kernel, grid=(rows // TILE,), out_shape=[out(width),...  35.3 us
    pallas_call x1, Pallas kernels, weights_all(): pl.pallas_call(functools.partial(weights_kernel, tuple(plan)), grid=(firs...  25.1 us

profile of v2, /device:TPU:0, one launch (start us, length us, event | category | flops | bytes accessed | tf_op | source)
XLA Modules:
  0.0 263.6 jit_solution(6937421233170994711)
XLA Ops:
  0.6 0.0 copy-start
  0.7 1.1 fusion.20
  1.7 0.9 copy.35
  2.7 0.7 pad_maximum_fusion.wqd
  3.4 1.8 copy.36
  5.2 1.3 broadcast_in_dim.43.qb_ref
  6.5 92.2 %mixed_all.1 = (bf16[2048,1024]{1,0:T(8,128)(2,1)}, bf16[2048,1024]{1,0:T(8,128)(2,1)}, bf16[2048,1024]{1,0:T(8,128)(2,1)}, bf16[2048,256]{1,0:T(8,128)(2,1)}, b...) custom-call(s32[2]{0:T(128)} %lim_ref.1, ...), custom_call_target="tpu_custom_call" | custom-call | flops 20000000000 | bytes 40000000 | tf_op jit(solution)/shard_map/mixed_all/pallas_call | solution.py:545
  98.7 35.3 %rows_all.1 = (bf16[2048,1024]{1,0:T(8,128)(2,1)}, bf16[2048,1024]{1,0:T(8,128)(2,1)}, bf16[2048,1024]{1,0:T(8,128)(2,1)}, bf16[2048,1024]{1,0:T(8,128)(2,1)}, b...) custom-call(bf16[2048,1024]{1,0:T(8,128)(2,1)} %get-tuple-element.33.x_ref, bf16[2048,1024]{1,0:T(8,128)(2,1)} %get-tuple-element.34.dyb_ref, ...), custom_call_target="tpu_custom_call" | custom-call | flops 20000000000 | bytes 30000000 | tf_op jit(solution)/shard_map/rows_all/pallas_call | solution.py:626
  134.1 0.0 copy-start.7
  134.1 0.0 copy-start.8
  134.1 25.1 %weights_all.1.blocks = bf16[192,128,128]{2,1,0:T(8,128)(2,1)} custom-call(bf16[2048,1024]{1,0:T(8,128)(2,1)} %get-tuple-element.31.h1_ref, bf16[2048,256]{1,0:T(8,128)(2,1)} %get-tuple-element.32.ctx_ref, bf16[2048,1024]{1,0:T(8,128)(2,1)} %get-tuple-element.39.h2_ref, bf16[2048,1024]{1,0:T(8,128)(2,1)} %get-tuple-element.40.act_ref, ...), custom_call_target="tpu_custom_call" | custom-call | flops 12999999488 | bytes 30000000 | tf_op jit(solution)/shard_map/weights_all/pallas_call | solution.py:674
  159.1 0.0 copy-done.7
  159.1 0.0 copy-done.8
  159.1 0.6 add.102.small
  159.8 0.8 fusion.18
  160.5 0.7 select_reduce_fusion.order
  161.2 0.0 copy-start.10
  161.2 0.0 copy-start.11
  161.2 0.0 copy-start.9
  161.2 0.0 copy-start.2
  161.2 79.5 %sums_all.1 = (f32[24,128,128]{2,1,0:T(8,128)}, f32[512,1024]{1,0:T(8,128)}, f32[512,1024]{1,0:T(8,128)}, f32[8,1024]{1,0:T(8,128)}) custom-call(s32[192]{0:T(256)} %select_reduce_fusion.order, bf16[192,128,128]{2,1,0:T(8,128)(2,1)} %weights_all.1.blocks, bf16[2048,1024]{1,0:T(8,128)(2,1)} %get-tuple-element.42.br, bf16[2048,1024]{1,0:T(8,128)(2,1)} %get-tuple-element.43.e, ...), custom_call_target="tpu_custom_call" | custom-call | bytes 30000000 | tf_op jit(solution)/shard_map/sums_all/pallas_call | solution.py:895
  240.7 0.0 copy-start.3
  240.7 0.9 broadcast_multiply_fusion
  241.6 0.0 copy-done.10
  241.7 0.6 rsqrt_multiply_fusion.1
  242.3 0.0 copy-done.11
  242.3 0.6 rsqrt_multiply_fusion.2
  242.9 0.0 copy-done.9
  242.9 0.6 rsqrt_multiply_fusion
  243.5 0.0 copy-done.2
  243.6 0.2 convert_reduce_fusion
  243.8 0.0 copy-start.13
  243.8 0.0 copy-start.12
  243.8 0.4 fusion.8
  244.2 0.0 copy-done.3
  244.2 0.7 fusion.19
  245.0 0.0 copy-done.13
  245.0 0.1 fusion.12
  245.1 0.0 copy-done.12
  245.1 0.0 copy-start.1
  245.1 4.3 %fusion.7 = (f32[512,1024]{1,0:T(8,128)}, bf16[512,1024]{1,0:T(8,128)(2,1)}) fusion(bf16[512,1024]{1,0:T(8,128)(2,1)S(1)} %copy-done.2, f32[512,1024]{1,0:T(8,128)} %get-tuple-element.47, bf16[512,1024]{1,0:T(8,128)(2,1)} %dy.1, f32[512]{0:T(512)S(1)} %get-tuple-element.71, f32[512]{0:T(512)S(1)} %get-tuple-element.72, f32[512]{0:T(512)S(1)} %add_rsqrt_fusion, ...), kind=kLoop, calls=%fused_computation.10 | loop fusion | flops 7340032 | bytes 9455616 | tf_op jit(solution)/shard_map/add | solution.py:967
  249.4 0.0 copy-done
  249.4 0.0 copy-done.1
  249.4 0.0 copy-start.4
  249.4 1.6 fusion.23
  251.0 0.0 copy-done.4
  251.0 0.0 copy-start.5
  251.0 2.9 %convolution_multiply_fusion = f32[24,128,128]{2,1,0:T(8,128)} fusion(f32[24,128,128]{1,2,0:T(8,128)S(1)} %fusion.23, f32[24,128,128]{2,1,0:T(8,128)S(1)} %copy-done.4), kind=kOutput, calls=%fused_computation.17 | convolution fusion | flops 604372992 | bytes 4718592 | tf_op jit(solution)/shard_map/sij,sjk->sik/dot_general | solution.py:980
  253.9 0.0 copy-done.5
  253.9 0.0 copy-start.6
  253.9 4.0 %add_multiply_fusion = f32[24,128,128]{2,1,0:T(8,128)} fusion(f32[24,128,128]{2,1,0:T(8,128)S(1)} %copy-done.5, f32[24,128,128]{2,1,0:T(8,128)S(1)} %copy-done.1), kind=kOutput, calls=%fused_computation.15 | convolution fusion | flops 604766208 | bytes 4718592 | tf_op jit(solution)/shard_map/sji,sjk->sik/dot_general | solution.py:976
  257.9 0.0 copy-done.6
  257.9 4.6 %add_multiply_fusion.1 = f32[24,128,128]{2,1,0:T(8,128)} fusion(f32[24,128,128]{2,1,0:T(8,128)S(1)} %copy-done.6, f32[24,128,128]{2,1,0:T(8,128)S(1)} %copy-done.1), kind=kOutput, calls=%fused_computation.16 | convolution fusion | flops 604766208 | bytes 4718592 | tf_op jit(solution)/shard_map/sij,skj->sik/dot_general | solution.py:973
  262.5 1.1 copy.40
  (9 shorter events, 0.1 us)
Async XLA Ops:
  0.6 248.8 %copy-start = (f32[24,128,128]{2,1,0:T(8,128)S(1)}, f32[24,128,128]{2,1,0:T(8,128)}, u32[]{:S(2)}) copy-start(f32[24,128,128]{2,1,0:T(8,128)} %param.34) | copy-start | bytes 4718596
  134.1 25.1 %copy-start.7 = (f32[8,1024]{1,0:T(8,128)S(1)}, f32[8,1024]{1,0:T(8,128)}, u32[]{:S(2)}) copy-start(f32[8,1024]{1,0:T(8,128)} %get-tuple-element.44) | copy-start | bytes 98308
  134.1 25.1 %copy-start.8 = (f32[8,1024]{1,0:T(8,128)S(1)}, f32[8,1024]{1,0:T(8,128)}, u32[]{:S(2)}) copy-start(f32[8,1024]{1,0:T(8,128)} %get-tuple-element.45) | copy-start | bytes 98308
  161.2 80.4 %copy-start.10 = (f32[1024]{0:T(1024)S(1)}, f32[1024]{0:T(1024)}, u32[]{:S(2)}) copy-start(f32[1024]{0:T(1024)} %param.38) | copy-start | bytes 12292
  161.2 81.1 %copy-start.11 = (f32[768]{0:T(1024)S(1)}, f32[768]{0:T(1024)}, u32[]{:S(2)}) copy-start(f32[768]{0:T(1024)} %param.37) | copy-start | bytes 9220
  161.2 81.7 %copy-start.9 = (f32[6,1024]{1,0:T(8,128)S(1)}, f32[6,1024]{1,0:T(8,128)}, u32[]{:S(2)}) copy-start(f32[6,1024]{1,0:T(8,128)} %param.36) | copy-start | bytes 73732
  161.2 82.3 %copy-start.2 = (bf16[512,1024]{1,0:T(8,128)(2,1)S(1)}, bf16[512,1024]{1,0:T(8,128)(2,1)}, u32[]{:S(2)}) copy-start(bf16[512,1024]{1,0:T(8,128)(2,1)} %x.1) | copy-start | bytes 3145732
  240.7 3.5 %copy-start.3 = (f32[512,1024]{1,0:T(8,128)S(1)}, f32[512,1024]{1,0:T(8,128)}, u32[]{:S(2)}) copy-start(f32[512,1024]{1,0:T(8,128)} %get-tuple-element.47) | copy-start | bytes 6291460
  243.8 1.2 copy-start.13
  243.8 1.3 copy-start.12
  245.1 4.3 %copy-start.1 = (f32[24,128,128]{2,1,0:T(8,128)S(1)}, f32[24,128,128]{2,1,0:T(8,128)}, u32[]{:S(2)}) copy-start(f32[24,128,128]{2,1,0:T(8,128)} %get-tuple-element.87) | copy-start | bytes 4718596
  249.4 1.6 copy-start.4
  251.0 2.9 %copy-start.5 = (f32[24,128,128]{2,1,0:T(8,128)S(1)}, f32[24,128,128]{2,1,0:T(8,128)}, u32[]{:S(2)}) copy-start(f32[24,128,128]{2,1,0:T(8,128)} %param.33) | copy-start | bytes 4718596
  253.9 4.0 %copy-start.6 = (f32[24,128,128]{2,1,0:T(8,128)S(1)}, f32[24,128,128]{2,1,0:T(8,128)}, u32[]{:S(2)}) copy-start(f32[24,128,128]{2,1,0:T(8,128)} %param.32) | copy-start | bytes 4718596

commit v3 on v2

--- a/solution.py
+++ b/solution.py
@@ -14,10 +14,10 @@
 LEN = 1024
 BLOCK = 128
 TILE = 256
+WIDE = 512
 MESH = pl.DeviceIdType.MESH
 VMEM_LIMIT = 60 * 1024 * 1024
 
-highest = lax.Precision.HIGHEST
 masked_score = -1e30
 shampoo_rate = 0.03
 adagrad_rate = 0.1
@@ -26,11 +26,6 @@
 bf16 = jnp.bfloat16
 
 
-def adagrad_step(grad_vec, accum):
-    accum_next = accum + grad_vec * grad_vec
-    return (accum_next, -adagrad_rate * grad_vec * lax.rsqrt(accum_next))
-
-
 def rotary_rows():
     half = ROT // 2
     inverse = np.power(np.float32(10000.0), -(np.arange(half, dtype=np.float32) * np.float32(2.0 / ROT)))
@@ -62,6 +57,14 @@
         @pl.loop(first, last)
         def _(hop):
             body(hop)
+
+
+def as_rows(vec):
+    return vec.reshape(-1, BLOCK)
+
+
+def as_line(rows):
+    return jnp.concatenate([rows[k : k + 1, :] for k in range(rows.shape[0])], axis=1)
 
 
 class Ring:
@@ -305,7 +308,7 @@
         cols = pl.ds(pl.multiple_of(i * TILE, TILE), TILE)
         begin = pl.multiple_of(pair * half_cols, BLOCK)
         proj = dot_nn(h1s[rows, :], wf[:, pl.ds(begin, pair_cols)])
-        proj = proj + qb_ref[:, pl.ds(pl.multiple_of(pair * pair_cols, BLOCK), pair_cols)]
+        proj = proj + as_line(qb_ref[pl.ds(pair * (pair_cols // BLOCK), pair_cols // BLOCK), :])
         proj = proj.T
         dctx = dot_nn(dyf[rows, :], wf[:, pl.ds(begin + pair_cols, 2 * HEAD)]).T
         cosine, sine = rot_ref[0:8, cols], rot_ref[8:16, cols]
@@ -349,8 +352,8 @@
         context = total[:HEAD] * inverse
         ctt[hh, :, here] = context
         grad = dct[hh, :, here].astype(f32)
-        delta = jnp.sum(grad * context, axis=0, keepdims=True) * inverse
         grad = (grad * inverse).astype(bf16)
+        delta = jnp.sum(grad.astype(f32) * context, axis=0, keepdims=True)
         dq = None
         for n, (c, p) in enumerate(zip(chunks, probs)):
             dp = dot_nn(vr[hh, c, :], grad)
@@ -536,7 +539,7 @@
 def mixed_all(count, limits, gains, biases, qkv_bias, rot, x, dy, wqd, w1, w2):
     far = count // 2
     rows, width = 4 * x.shape[0], x.shape[1]
-    ctx_cols, proj_cols = 4 * HEAD, qkv_bias.shape[1]
+    ctx_cols, proj_cols = 4 * HEAD, qkv_bias.size
     out = lambda r, c: jax.ShapeDtypeStruct((r, c), bf16)
     full = lambda v: out(count * v.shape[0], v.shape[1])
     any_, vmem = pl.BlockSpec(memory_space=pl.ANY), pl.BlockSpec(memory_space=pltpu.VMEM)
@@ -576,111 +579,115 @@
     return x * phi, phi + x * bell * (1.0 / math.sqrt(2.0 * math.pi))
 
 
-def rows_kernel(
-    x_ref, dyb_ref, ctx_ref, dproj_ref, wqd_ref, w1_ref, w2_ref, gain_ref, bias_ref, fb_ref,
-    h2_ref, act_ref, dab_ref, br_ref, e_ref, sum_ref,
+def hidden_kernel(
+    gain_ref, bias_ref, fb_ref, x, h1, dyb, ctx, dproj, w1, w2,
+    act_out, dab_out, g_out, sum_ref,
+    xs, h1s, dys, cs, ps, w1s, w2s, h2s, acts, dabs, gs, sem, osem, gsem,
 ):
-    @pl.when(pl.program_id(0) == 0)
-    def _():
-        sum_ref[...] = jnp.zeros_like(sum_ref)
-
-    xhat, _ = normed(x_ref[...].astype(f32))
-    h2 = (xhat * gain_ref[1:2, :] + bias_ref[1:2, :]).astype(bf16)
-    h2_ref[...] = h2
-    pre = dot_nn(h2, w1_ref[...]) + fb_ref[...]
-    act, slope = gelu_both(pre)
-    act = act.astype(bf16)
-    act_ref[...] = act
-    dab = (dot_nn(dyb_ref[...], w2_ref[...]) * slope).astype(bf16)
-    dab_ref[...] = dab
-    br = dot_nt(act, w2_ref[...])
-    dh2 = dot_nt(dab, w1_ref[...])
-    dh1 = None
-    wide, thin = 6 * HEAD, 2 * HEAD
-    for p in range(2):
-        lo = p * (wide + thin)
-        br = br + dot_nt(ctx_ref[:, p * thin : (p + 1) * thin], wqd_ref[:, lo + wide : lo + wide + thin])
-        part = dot_nt(dproj_ref[:, p * wide : (p + 1) * wide], wqd_ref[:, lo : lo + wide])
-        dh1 = part if dh1 is None else dh1 + part
-    br_ref[...] = br.astype(bf16)
-    e_ref[...] = (dh1 * gain_ref[0:1, :] + dh2 * gain_ref[1:2, :]).astype(bf16)
-    total = lambda v: jnp.sum(v, axis=0, keepdims=True)
-    sum_ref[0:1, :] += total(dh1 * xhat)
-    sum_ref[1:2, :] += total(dh2 * xhat)
-    sum_ref[2:3, :] += total(dh1)
-    sum_ref[3:4, :] += total(dh2)
-    sum_ref[6:7, :] += total(dab.astype(f32))
-
-
-def rows_all(xf, dyb, ctx, dproj, wqdf, w1f, w2f, gains, biases, fc1_bias):
-    rows, width = xf.shape
-
-    def tile(cols):
-        return pl.BlockSpec((TILE, cols), lambda s: (s, 0))
-
-    def whole(v):
-        return pl.BlockSpec(v.shape, lambda s: (0, 0))
-
-    out = lambda cols: jax.ShapeDtypeStruct((rows, cols), bf16)
-    hidden = w1f.shape[1]
-    return pl.pallas_call(
-        rows_kernel,
-        grid=(rows // TILE,),
-        out_shape=[out(width), out(hidden), out(hidden), out(width), out(width)]
-        + [jax.ShapeDtypeStruct((8, width), f32)],
-        in_specs=[tile(v.shape[1]) for v in (xf, dyb, ctx, dproj)]
-        + [whole(v) for v in (wqdf, w1f, w2f, gains, biases, fc1_bias)],
-        out_specs=[tile(width), tile(hidden), tile(hidden), tile(width), tile(width)]
-        + [pl.BlockSpec((8, width), lambda s: (0, 0))],
-        compiler_params=pltpu.CompilerParams(vmem_limit_bytes=VMEM_LIMIT),
-        cost_estimate=pl.CostEstimate(flops=int(2e10), bytes_accessed=int(3e7), transcendentals=int(4e6)),
-        name="rows_all",
-    )(xf, dyb, ctx, dproj, wqdf, w1f, w2f, gains, biases, fc1_bias)
-
-
-def weights_kernel(plan, h1_ref, ctx_ref, h2_ref, act_ref, dproj_ref, dyb_ref, dab_ref, g_ref):
-    job = pl.program_id(0)
-    lefts = (h1_ref, ctx_ref, h2_ref, act_ref)
-    rights = (dproj_ref, dyb_ref, dab_ref, dyb_ref)
-    for kind, (first, jobs, base, per_row) in enumerate(plan):
-
-        @pl.when((job >= first) & (job < first + jobs))
-        def _():
-            grad = dot_tn(lefts[kind][...], rights[kind][...]).astype(bf16)
-            start = base + (job - first) * (TILE // BLOCK) * per_row
-            for r in range(TILE // BLOCK):
+    rows = x.shape[0]
+    tiles = rows // WIDE
+
+    def tile_copy(k, src, dst, i):
+        at = pl.ds(pl.multiple_of(i * WIDE, WIDE), WIDE)
+        return pltpu.make_async_copy(src.at[at], dst.at[at], sem.at[k, i])
+
+    def whole(k, src, dst):
+        return pltpu.make_async_copy(src, dst, sem.at[k, 0])
+
+    whole(0, w1, w1s).start()
+    tile_copy(2, x, xs, 0).start()
+    whole(1, w2, w2s).start()
+    tile_copy(3, dyb, dys, 0).start()
+    for i in range(1, tiles):
+        tile_copy(2, x, xs, i).start()
+        tile_copy(3, dyb, dys, i).start()
+    late = [whole(4, h1, h1s), whole(5, ctx, cs), whole(6, dproj, ps)]
+    for copy in late:
+        copy.start()
+    sum_ref[...] = jnp.zeros_like(sum_ref)
+    whole(0, w1, w1s).wait()
+
+    def save(k, src, dst, i):
+        at = pl.ds(pl.multiple_of(i * WIDE, WIDE), WIDE)
+        return pltpu.make_async_copy(src.at[at], dst.at[at], osem.at[k, i])
+
+    @pl.loop(0, tiles)
+    def _(i):
+        at = pl.ds(pl.multiple_of(i * WIDE, WIDE), WIDE)
+        tile_copy(2, x, xs, i).wait()
+        xhat, _ = normed(xs[at, :].astype(f32))
+        h2 = (xhat * gain_ref[1:2, :] + bias_ref[1:2, :]).astype(bf16)
+        h2s[at, :] = h2
+        pre = dot_nn(h2, w1s[...]) + as_line(fb_ref[...])
+        act, slope = gelu_both(pre)
+        acts[at, :] = act.astype(bf16)
+        save(0, acts, act_out, i).start()
+
+        @pl.when(i == 0)
+        def _():
+            whole(1, w2, w2s).wait()
+
+        tile_copy(3, dyb, dys, i).wait()
+        dab = (dot_nn(dys[at, :], w2s[...]) * slope).astype(bf16)
+        dabs[at, :] = dab
+        save(1, dabs, dab_out, i).start()
+        sum_ref[6:7, :] += jnp.sum(dab.astype(f32), axis=0, keepdims=True)
+
+    for copy in late:
+        copy.wait()
+    base, spans = 0, []
+    for kind, (left, right) in enumerate(((h1s, ps), (cs, dys), (h2s, dabs), (acts, dys))):
+        tall = min(WIDE, left.shape[1])
+        jobs, per_row = left.shape[1] // tall, right.shape[1] // BLOCK
+        count = tall // BLOCK * per_row
+
+        @pl.loop(0, jobs)
+        def _(j):
+            grad = dot_tn(left[:, pl.ds(pl.multiple_of(j * tall, tall), tall)], right[...]).astype(bf16)
+            start = base + j * count
+            for r in range(tall // BLOCK):
                 for c in range(per_row):
-                    g_ref[start + r * per_row + c] = grad[
+                    gs[start + r * per_row + c] = grad[
                         r * BLOCK : (r + 1) * BLOCK, c * BLOCK : (c + 1) * BLOCK
                     ]
 
-
-def weights_all(h1, ctx, h2, act, dproj, dyb, dab):
-    rows = h1.shape[0]
-    lefts, rights = (h1, ctx, h2, act), (dproj, dyb, dab, dyb)
-    plan, first, base = [], 0, 0
-    for left, right in zip(lefts, rights):
-        jobs, per_row = left.shape[1] // TILE, right.shape[1] // BLOCK
-        plan.append((first, jobs, base, per_row))
-        first, base = first + jobs, base + jobs * (TILE // BLOCK) * per_row
-
-    def tile(kind):
-        begin, jobs = plan[kind][:2]
-        return pl.BlockSpec((rows, TILE), lambda j: (0, jnp.clip(j - begin, 0, jobs - 1)))
-
-    def whole(v):
-        return pl.BlockSpec(v.shape, lambda j: (0, 0))
-
+        span = pl.ds(base, jobs * count)
+        spans.append(pltpu.make_async_copy(gs.at[span], g_out.at[span], gsem.at[kind]))
+        spans[-1].start()
+        base += jobs * count
+    for copy in spans:
+        copy.wait()
+    for i in range(tiles):
+        save(0, acts, act_out, i).wait()
+        save(1, dabs, dab_out, i).wait()
+
+
+def hidden_all(x, h1, dyb, ctx, dproj, w1, w2, gains, biases, fc1_bias):
+    rows, width = x.shape
+    hidden = w1.shape[1]
+    blocks = (width * (dproj.shape[1] + hidden) + (ctx.shape[1] + hidden) * width) // (BLOCK * BLOCK)
+    any_, vmem = pl.BlockSpec(memory_space=pl.ANY), pl.BlockSpec(memory_space=pltpu.VMEM)
+    like = lambda v: pltpu.VMEM(v.shape, v.dtype)
+    tiles = rows // WIDE
     return pl.pallas_call(
-        functools.partial(weights_kernel, tuple(plan)),
-        grid=(first,),
-        out_shape=jax.ShapeDtypeStruct((base, BLOCK, BLOCK), bf16),
-        in_specs=[tile(k) for k in range(4)] + [whole(dproj), whole(dyb), whole(dab)],
-        out_specs=pl.BlockSpec((base, BLOCK, BLOCK), lambda j: (0, 0, 0)),
+        hidden_kernel,
+        out_shape=[
+            jax.ShapeDtypeStruct((rows, hidden), bf16), jax.ShapeDtypeStruct((rows, hidden), bf16),
+            jax.ShapeDtypeStruct((blocks, BLOCK, BLOCK), bf16), jax.ShapeDtypeStruct((8, width), f32),
+        ],
+        in_specs=[vmem] * 3 + [any_] * 7,
+        out_specs=[any_] * 3 + [vmem],
+        scratch_shapes=[like(v) for v in (x, h1, dyb, ctx, dproj, w1, w2)]
+        + [
+            pltpu.VMEM((rows, width), bf16), pltpu.VMEM((rows, hidden), bf16), pltpu.VMEM((rows, hidden), bf16),
+            pltpu.VMEM((blocks, BLOCK, BLOCK), bf16),
+            pltpu.SemaphoreType.DMA((7, tiles)), pltpu.SemaphoreType.DMA((2, tiles)),
+            pltpu.SemaphoreType.DMA((4,)),
+        ],
         compiler_params=pltpu.CompilerParams(vmem_limit_bytes=VMEM_LIMIT),
-        cost_estimate=pl.CostEstimate(flops=int(1.3e10), bytes_accessed=int(3e7), transcendentals=0),
-        name="weights_all",
-    )(h1, ctx, h2, act, dproj, dyb, dab)
+        cost_estimate=pl.CostEstimate(flops=int(2.2e10), bytes_accessed=int(4e7), transcendentals=int(4e6)),
+        name="hidden_all",
+    )(gains, biases, fc1_bias, x, h1, dyb, ctx, dproj, w1, w2)
 
 
 class Scatter:
@@ -693,10 +700,10 @@
     def index(self, half, way, hop):
         return (half * 2 + way) * self.far + hop - 1
 
-    def copy(self, half, way, hop):
+    def copy(self, half, way, hop, first):
         i = self.index(half, way, hop)
         return pltpu.make_async_remote_copy(
-            src_ref=self.sbuf.at[i],
+            src_ref=self.sbuf.at[half * 2 + way] if first else self.rbuf.at[i - 1],
             dst_ref=self.rbuf.at[i],
             send_sem=self.send.at[i],
             recv_sem=self.recv.at[i],
@@ -707,28 +714,30 @@
     def own(self, dest, half, k):
         return self.blocks[self.order[dest * self.per + k], half * 64 : half * 64 + 64, :].astype(f32)
 
-    def step(self, half, way, hop, hops, first):
+    def step(self, half, way, hop, first):
+        hops = hop_count(half, way, self.ring.count)
         dest = self.ring.at((hops + 1 - hop) if way == 0 else (hop - hops - 1))
         i = self.index(half, way, hop)
         if not first:
-            self.copy(half, way, hop - 1).wait_recv()
+            self.copy(half, way, hop - 1, True).wait_recv()
 
         def one(k, carry):
             value = self.own(dest, half, k)
-            if not first:
-                value = value + self.rbuf[i - 1, k].astype(f32)
-            self.sbuf[i, k] = value.astype(bf16)
+            if first:
+                self.sbuf[half * 2 + way, k] = value.astype(bf16)
+            else:
+                self.rbuf[i - 1, k] = (value + self.rbuf[i - 1, k].astype(f32)).astype(bf16)
             return carry
 
         lax.fori_loop(0, self.per, one, 0)
-        self.copy(half, way, hop).start()
+        self.copy(half, way, hop, first).start()
 
     def last(self, half, scale):
         came = []
         for way in range(2):
             hops = hop_count(half, way, self.ring.count)
             if hops >= 1:
-                self.copy(half, way, hops).wait_recv()
+                self.copy(half, way, hops, True).wait_recv()
                 came.append(self.index(half, way, hops))
         me = self.ring.me
 
@@ -745,21 +754,19 @@
         for half in range(2):
             for way in range(2):
                 hops = hop_count(half, way, self.ring.count)
-                for_hops(1, hops + 1, lambda hop: self.copy(half, way, hop).wait_send(), self.ring.count)
+                for_hops(
+                    1, hops + 1, lambda hop: self.copy(half, way, hop, True).wait_send(), self.ring.count
+                )
 
 
 class RowSum:
-    def __init__(self, part, out, r1, s2, r2, send, recv):
+    def __init__(self, parts, out, r1, r2, send, recv):
         self.tensor = lax.axis_index("tensor")
         self.dp = lax.axis_index("dp")
         self.near = self.tensor + 1 - 2 * (self.tensor % 2)
         self.across = (self.tensor + 2) % 4
-        self.part, self.out, self.r1, self.s2, self.r2 = part, out, r1, s2, r2
+        self.parts, self.out, self.r1, self.r2 = parts, out, r1, r2
         self.send, self.recv = send, recv
-        self.rows = out.shape[0]
-
-    def slot(self, owner):
-        return self.part.at[pl.ds(pl.multiple_of(owner * self.rows, 16), self.rows)]
 
     def remote(self, src, dst, sem, device):
         return pltpu.make_async_remote_copy(
@@ -768,43 +775,43 @@
         )
 
     def pair(self, k):
-        owner = (self.near + 2) % 4 if k == 0 else self.near
-        return self.remote(self.slot(owner), self.r1.at[k], k, self.near)
+        return self.remote(self.parts.at[2 * k], self.r1.at[k], k, self.near)
 
     def cross(self):
-        return self.remote(self.s2, self.r2, 2, self.across)
-
-    def begin(self):
-        self.pair(0).start()
-        self.pair(1).start()
+        return self.remote(self.parts.at[1], self.r2, 2, self.across)
 
     def middle(self):
         self.pair(0).wait_recv()
-        self.s2[...] = (self.slot(self.across)[...].astype(f32) + self.r1[0].astype(f32)).astype(bf16)
-        self.cross().start()
+        self.parts[1] = (self.parts[1].astype(f32) + self.r1[0].astype(f32)).astype(bf16)
 
     def end(self):
         self.pair(1).wait_recv()
         self.cross().wait_recv()
-        self.out[...] = (
-            self.slot(self.tensor)[...].astype(f32) + self.r1[1].astype(f32) + self.r2[...].astype(f32)
-        )
+        self.out[...] = self.parts[3].astype(f32) + self.r1[1].astype(f32) + self.r2[...].astype(f32)
+
+    def finish(self):
         self.pair(0).wait_send()
         self.pair(1).wait_send()
         self.cross().wait_send()
 
 
 def sums_kernel(
-    count, scale, order, blocks, br, e, small, grad, br_sum, e_sum, small_sum,
-    sbuf, rbuf, r1, s2, r2, t_in, d_in, d_out, ss, sr, rs, rr, ts, tr, ds, dr,
+    count, scale, order, gain_ref, small_a, small_b, g_hbm, x, act, dab, ctx, dproj, wqd, w1, w2,
+    grad, small_sum, br_out, e_out,
+    gbuf, sbuf, rbuf, xs, acts, dabs, cs, ps, wqds, w1s, w2s, parts, r1, r2, tot, small, t_in, d_in, d_out,
+    ss, sr, rs, rr, ts, tr, ds, dr, ls, ws, os,
 ):
     ring = Ring(count)
     me, tensor = ring.me, ring.tensor
-    scatter = Scatter(ring, order, blocks, grad, sbuf, rbuf, ss, sr)
+    rows = r2.shape[1]
+    load_g = pltpu.make_async_copy(g_hbm, gbuf, ws.at[0])
+    load_g.start()
+    scatter = Scatter(ring, order, gbuf, grad, sbuf, rbuf, ss, sr)
     sums = [
-        RowSum(part, out, r1.at[n], s2.at[n], r2.at[n], rs.at[n], rr.at[n])
-        for n, (part, out) in enumerate(((br, br_sum), (e, e_sum)))
+        RowSum(parts.at[n], tot.at[n], r1.at[n], r2.at[n], rs.at[n], rr.at[n]) for n in range(2)
     ]
+    near, across = sums[0].near, sums[0].across
+    owners = ((near + 2) % 4, across, near, tensor)
 
     def t_copy(step):
         return pltpu.make_async_remote_copy(
@@ -826,58 +833,125 @@
     def _(step):
         pl.semaphore_signal(barrier, inc=1, device_id=((me + step) % count, tensor), device_id_type=MESH)
 
+    weights = [
+        pltpu.make_async_copy(src, dst, ws.at[1 + k])
+        for k, (src, dst) in enumerate(((w2, w2s), (w1, w1s), (wqd, wqds)))
+    ]
+
+    def load(n):
+        at = pl.ds(pl.multiple_of(owners[n] * rows, 16), rows)
+        return [
+            pltpu.make_async_copy(src.at[at], dst.at[n % 2], ls.at[k, n % 2])
+            for k, (src, dst) in enumerate(((x, xs), (act, acts), (dab, dabs), (ctx, cs), (dproj, ps)))
+        ]
+
+    far = count // 2
+    first, second = ((0, 0), (1, 1)), ((1, 0), (0, 1))
+    load_g.wait()
     pl.semaphore_wait(barrier, 3 + count - 1)
-
-    far = count // 2
-    for half in range(2):
-        for way in (half, 1 - half):
-            hops = hop_count(half, way, count)
-            if hops >= 1:
-                scatter.step(half, way, 1, hops, True)
+    for half, way in first + second:
+        if hop_count(half, way, count) >= 1:
+            scatter.step(half, way, 1, True)
+    for copy in weights + load(0):
+        copy.start()
+    small[...] = small_a[...] + small_b[...]
+
+    def ring_step(hop, which):
+        for half, way in which:
+            if which is first:
+                scatter.step(half, way, hop, False)
+            else:
+
+                @pl.when(hop <= far - 1)
+                def _():
+                    scatter.step(half, way, hop, False)
+
+    wide, thin = 6 * HEAD, 2 * HEAD
+    total = lambda v: jnp.sum(v, axis=0, keepdims=True)
+
+    def work(n, r):
+        slot, at = n % 2, slice(r * TILE, (r + 1) * TILE)
+        br = dot_nt(acts[slot, at, :], w2s[...])
+        dh1 = None
+        for p in range(2):
+            lo = p * (wide + thin)
+            br = br + dot_nt(cs[slot, at, p * thin : (p + 1) * thin], wqds[:, lo + wide : lo + wide + thin])
+            part = dot_nt(ps[slot, at, p * wide : (p + 1) * wide], wqds[:, lo : lo + wide])
+            dh1 = part if dh1 is None else dh1 + part
+        parts[0, n, at, :] = br.astype(bf16)
+        dh2 = dot_nt(dabs[slot, at, :], w1s[...])
+        xhat, _ = normed(xs[slot, at, :].astype(f32))
+        parts[1, n, at, :] = (dh1 * gain_ref[0:1, :] + dh2 * gain_ref[1:2, :]).astype(bf16)
+        small[0:1, :] += total(dh1 * xhat)
+        small[1:2, :] += total(dh2 * xhat)
+        small[2:3, :] += total(dh1)
+        small[3:4, :] += total(dh2)
+
+    for n in range(4):
+        if n < 3:
+            for copy in load(n + 1):
+                copy.start()
+        if n == 0:
+            for copy in weights:
+                copy.wait()
+        for copy in load(n):
+            copy.wait()
+        for r in range(rows // TILE):
+            work(n, r)
+        if n in (0, 2):
+            for s in sums:
+                s.pair(n // 2).start()
+        if n == 1:
+            for s in sums:
+                s.middle()
+            sums[0].cross().start()
+            if far >= 2 and count <= 8:
+                ring_step(2, first)
+        if n == 3 and far >= 2 and count <= 8:
+            ring_step(2, second)
+
     for step in range(1, 4):
         t_copy(step).start()
-    for s in sums:
-        s.begin()
-    sums[0].middle()
+    sums[1].cross().start()
+
+    def both(hop):
+        ring_step(hop, first)
+        ring_step(hop, second)
+
+    if count <= 8:
+        both(3)
+    else:
+        for_hops(2, far + 1, both, count)
     for step in range(1, 4):
         t_copy(step).wait_recv()
     t_in[tensor] = small[...]
     row = lax.broadcasted_iota(jnp.int32, small.shape, 0)
-    total = t_in[0] + t_in[1] + t_in[2] + t_in[3]
-    d_out[...] = jnp.where(row < 4, total, small[...])
+    summed = t_in[0] + t_in[1] + t_in[2] + t_in[3]
+    d_out[...] = jnp.where(row < 4, summed, small[...])
 
     @pl.loop(1, count)
     def _(step):
         d_copy(step).start()
 
-    def ring_step(hop):
-        for half in range(2):
-            for way in (half, 1 - half):
-                hops = hop_count(half, way, count)
-                if half == way:
-                    scatter.step(half, way, hop, hops, False)
-                else:
-
-                    @pl.when(hop <= hops)
-                    def _():
-                        scatter.step(half, way, hop, hops, False)
-
-    for_hops(2, far, ring_step, count)
-    sums[1].middle()
-    if far >= 2:
-        ring_step(far)
+    if count <= 8:
+        both(4)
     sums[0].end()
+    saves = [pltpu.make_async_copy(tot.at[n], out, os.at[n]) for n, out in enumerate((br_out, e_out))]
+    saves[0].start()
 
     @pl.loop(1, count)
     def _(step):
         d_copy(step).wait_recv()
 
     d_in[me] = d_out[...]
-    small_sum[...] = lax.fori_loop(1, count, lambda k, acc: acc + d_in[k], d_in[0])
+    small_sum[...] = scale * lax.fori_loop(1, count, lambda k, acc: acc + d_in[k], d_in[0])
     sums[1].end()
+    saves[1].start()
     for half in range(2):
         scatter.last(half, scale)
     scatter.finish()
+    for s in sums:
+        s.finish()
     for step in range(1, 4):
         t_copy(step).wait_send()
 
@@ -885,40 +959,134 @@
     def _(step):
         d_copy(step).wait_send()
 
-
-def sums_all(count, scale, order, blocks, br, e, small):
+    for copy in saves:
+        copy.wait()
+
+
+def sums_all(count, scale, order, gains, small, small_b, blocks, x, act, dab, ctx, dproj, wqd, w1, w2):
     per = blocks.shape[0] // count
-    rows, width = br.shape[0] // 4, br.shape[1]
+    rows, width = x.shape[0] // 4, x.shape[1]
     far = count // 2
-    vmem = pl.BlockSpec(memory_space=pltpu.VMEM)
+    any_, vmem = pl.BlockSpec(memory_space=pl.ANY), pl.BlockSpec(memory_space=pltpu.VMEM)
     dma = lambda *n: pltpu.SemaphoreType.DMA(n)
+    two = lambda v: pltpu.VMEM((2, rows, v.shape[1]), v.dtype)
+    like = lambda v: pltpu.VMEM(v.shape, v.dtype)
+    sum_shape = jax.ShapeDtypeStruct((rows, width), f32)
     return pl.pallas_call(
         functools.partial(sums_kernel, count, scale),
         out_shape=[
-            jax.ShapeDtypeStruct((per, BLOCK, BLOCK), f32),
-            jax.ShapeDtypeStruct((rows, width), f32),
-            jax.ShapeDtypeStruct((rows, width), f32),
-            jax.ShapeDtypeStruct(small.shape, f32),
+            jax.ShapeDtypeStruct((per, BLOCK, BLOCK), f32), jax.ShapeDtypeStruct(small.shape, f32),
+            sum_shape, sum_shape,
         ],
-        in_specs=[pl.BlockSpec(memory_space=pltpu.SMEM)] + [vmem] * 4,
-        out_specs=[vmem] * 4,
+        in_specs=[pl.BlockSpec(memory_space=pltpu.SMEM)] + [vmem] * 3 + [any_] * 9,
+        out_specs=[vmem, vmem, any_, any_],
         scratch_shapes=[
-            pltpu.VMEM((4 * far, per, 64, BLOCK), bf16),
-            pltpu.VMEM((4 * far, per, 64, BLOCK), bf16),
-            pltpu.VMEM((2, 2, rows, width), bf16),
-            pltpu.VMEM((2, rows, width), bf16),
-            pltpu.VMEM((2, rows, width), bf16),
-            pltpu.VMEM((4,) + small.shape, f32),
-            pltpu.VMEM((count,) + small.shape, f32),
-            pltpu.VMEM(small.shape, f32),
+            like(blocks),
+            pltpu.VMEM((4, per, 64, BLOCK), bf16), pltpu.VMEM((4 * far, per, 64, BLOCK), bf16),
+            two(x), two(act), two(dab), two(ctx), two(dproj), like(wqd), like(w1), like(w2),
+            pltpu.VMEM((2, 4, rows, width), bf16), pltpu.VMEM((2, 2, rows, width), bf16),
+            pltpu.VMEM((2, rows, width), bf16), pltpu.VMEM((2, rows, width), f32),
+            pltpu.VMEM(small.shape, f32), pltpu.VMEM((4,) + small.shape, f32),
+            pltpu.VMEM((count,) + small.shape, f32), pltpu.VMEM(small.shape, f32),
             dma(4 * far), dma(4 * far), dma(2, 3), dma(2, 3), dma(4), dma(4), dma(count), dma(count),
+            dma(5, 2), dma(4), dma(2),
         ],
         compiler_params=pltpu.CompilerParams(
             collective_id=1, has_side_effects=True, vmem_limit_bytes=VMEM_LIMIT
         ),
-        cost_estimate=pl.CostEstimate(flops=0, bytes_accessed=int(3e7), transcendentals=0),
+        cost_estimate=pl.CostEstimate(flops=int(1.3e10), bytes_accessed=int(4e7), transcendentals=0),
         name="sums_all",
-    )(order, blocks, br, e, small)
+    )(order, gains, small, small_b, blocks, x, act, dab, ctx, dproj, wqd, w1, w2)
+
+
+def finish_kernel(
+    steps, lim_ref, bias_ref, small_ref, racc_ref, qacc_ref, facc_ref, grad, tok, dy, br, e, ls, rs, lr, rr,
+    gout, out, dx, lout, rout, cout, racc, rupd, qacc, qupd, facc, fupd,
+    g_v, tok_v, dy_v, br_v, e_v, ls_v, rs_v, lr_v, rr_v, out_v, dx_v, lo_v, ro_v, co_v, isem, osem,
+):
+    tensor = lax.axis_index("tensor")
+    own_rows, blocks = tok.shape[0], grad.shape[0]
+    rows, some = own_rows // steps, blocks // steps
+    ins = [(grad, g_v), (ls, ls_v), (rs, rs_v), (lr, lr_v), (rr, rr_v), (tok, tok_v), (dy, dy_v), (br, br_v), (e, e_v)]
+    outs = [(g_v, gout), (lo_v, lout), (ro_v, rout), (co_v, cout), (out_v, out), (dx_v, dx)]
+
+    def span(ref, s):
+        size = ref.shape[0] // steps
+        return ref.at[pl.ds(s * size if ref.shape[0] == blocks else pl.multiple_of(s * size, 16), size)]
+
+    def fetch(k, s):
+        return pltpu.make_async_copy(span(ins[k][0], s), span(ins[k][1], s), isem.at[k, s])
+
+    def store(k, s):
+        return pltpu.make_async_copy(span(outs[k][0], s), span(outs[k][1], s), osem.at[k, s])
+
+    for s in range(steps):
+        for k in range(len(ins)):
+            fetch(k, s).start()
+    small = small_ref[...]
+
+    def adagrad(grad_vec, accum, new, update):
+        accum_next = accum + grad_vec * grad_vec
+        new[...] = accum_next
+        update[...] = -adagrad_rate * grad_vec * lax.rsqrt(accum_next)
+
+    def stacked(line, count):
+        return jnp.concatenate([line[:, k * BLOCK : (k + 1) * BLOCK] for k in range(count)], axis=0)
+
+    adagrad(jnp.concatenate([small[0:5], small[4:5]], axis=0), racc_ref[...], racc, rupd)
+    adagrad(stacked(small[5:6], qacc.shape[0]), qacc_ref[...], qacc, qupd)
+    adagrad(stacked(small[6:7], facc.shape[0]), facc_ref[...], facc, fupd)
+    shift = bias_ref[2:3, :] + bias_ref[3:4, :]
+
+    @pl.loop(0, steps)
+    def _(s):
+        for k in range(len(ins)):
+            fetch(k, s).wait()
+
+        for b in range(some):
+            k = s * some + b
+            low = g_v[k].astype(bf16)
+            lo_v[k] = stat_decay * ls_v[k] + (1.0 - stat_decay) * dot_nt(low, low)
+            ro_v[k] = stat_decay * rs_v[k] + (1.0 - stat_decay) * dot_tn(low, low)
+            pushed = dot_nn(lr_v[k].astype(bf16), low).astype(bf16)
+            co_v[k] = -shampoo_rate * dot_nn(pushed, rr_v[k].astype(bf16))
+
+        at = pl.ds(pl.multiple_of(s * rows, 16), rows)
+        x = tok_v[at, :].astype(f32)
+        out_v[at, :] = (x + br_v[at, :] + shift).astype(bf16)
+        start = tensor * own_rows + s * rows
+        place = start % LEN + lax.broadcasted_iota(jnp.int32, (rows, 1), 0)
+        kept = jnp.where(place < lim_ref[start // LEN], dy_v[at, :].astype(f32), 0.0)
+        xhat, scale = normed(x)
+        v = e_v[at, :]
+        dx_v[at, :] = kept + scale * (
+            v - jnp.mean(v, axis=-1, keepdims=True) - xhat * jnp.mean(v * xhat, axis=-1, keepdims=True)
+        )
+        for k in range(len(outs)):
+            store(k, s).start()
+
+    for s in range(steps):
+        for k in range(len(outs)):
+            store(k, s).wait()
+
+
+def finish_all(limits, biases, small, racc, qacc, facc, grad, tok, dy, br, e, ls, rs, lr, rr):
+    steps = 4 if grad.shape[0] % 4 == 0 else 1
+    any_, vmem = pl.BlockSpec(memory_space=pl.ANY), pl.BlockSpec(memory_space=pltpu.VMEM)
+    shape = lambda v: jax.ShapeDtypeStruct(v.shape, v.dtype)
+    like = lambda v: pltpu.VMEM(v.shape, v.dtype)
+    vectors = [racc, racc, qacc, qacc, facc, facc]
+    return pl.pallas_call(
+        functools.partial(finish_kernel, steps),
+        out_shape=[shape(grad), shape(tok), shape(e)] + [shape(grad)] * 3 + [shape(v) for v in vectors],
+        in_specs=[pl.BlockSpec(memory_space=pltpu.SMEM)] + [vmem] * 5 + [any_] * 9,
+        out_specs=[any_] * 6 + [vmem] * 6,
+        scratch_shapes=[like(v) for v in (grad, tok, dy, br, e, ls, rs, lr, rr, tok, e, ls, ls, ls)]
+        + [pltpu.SemaphoreType.DMA((9, steps)), pltpu.SemaphoreType.DMA((6, steps))],
+        compiler_params=pltpu.CompilerParams(vmem_limit_bytes=VMEM_LIMIT),
+        cost_estimate=pl.CostEstimate(flops=int(4e8), bytes_accessed=int(2e7), transcendentals=0),
+        name="finish_all",
+    )(limits, biases, small, racc, qacc, facc, grad, tok, dy, br, e, ls, rs, lr, rr)
 
 
 def shards(
@@ -931,7 +1099,6 @@
     tensor_rank = lax.axis_index("tensor")
     own_rows, width = tokens.shape
     group_rows = own_rows * tensor_count
-    group_seqs = seq_lengths.shape[0]
     grad_scale = 1.0 / math.sqrt(group_rows * dp_count)
     blocks_tensor = block_slot.shape[0] // tensor_count
     per_dev = blocks_tensor // dp_count
@@ -947,46 +1114,23 @@
         [qkv_weight[:, :wide], dense_turned[:, :thin], qkv_weight[:, wide:], dense_turned[:, thin:]], axis=1
     )
     xf, h1, dyb, ctx, dproj, wqdf, w1f, w2f, sum_a = mixed_all(
-        dp_count, seq_lengths, norm_gains, row_biases, qkv_bias[None], jnp.asarray(rotary_rows()),
+        dp_count, seq_lengths, norm_gains, row_biases, as_rows(qkv_bias), jnp.asarray(rotary_rows()),
         tokens, out_grad, wqd, fc1_weight, fc2_weight.T,
     )
-    h2, act, dab, br, e, sum_b = rows_all(
-        xf, dyb, ctx, dproj, wqdf, w1f, w2f, norm_gains, row_biases, fc1_bias[None]
+    act, dab, blocks, sum_b = hidden_all(
+        xf, h1, dyb, ctx, dproj, w1f, w2f, norm_gains, row_biases, as_rows(fc1_bias)
     )
-    blocks = weights_all(h1, ctx, h2, act, dproj, dyb, dab)
-    own_grad, branch, e_sum, small = sums_all(dp_count, grad_scale, order, blocks, br, e, sum_a + sum_b)
-
-    inputs = tokens.astype(f32)
-    layer_out = (inputs + branch + row_biases[2] + row_biases[3]).astype(bf16)
-    row_ids = tensor_rank * own_rows + jnp.arange(own_rows)
-    seq_match = (row_ids // LEN)[:, None] == jnp.arange(group_seqs)[None, :]
-    row_limit = jnp.sum(jnp.where(seq_match, seq_lengths[None, :], 0), axis=1)
-    row_valid = (row_ids % LEN < row_limit).astype(f32)
-    grad_out = out_grad.astype(f32) * row_valid[:, None]
-    xhat, scale = normed(inputs)
-    input_grad = grad_out + scale * (
-        e_sum
-        - jnp.mean(e_sum, axis=-1, keepdims=True)
-        - xhat * jnp.mean(e_sum * xhat, axis=-1, keepdims=True)
+    own_grad, small, branch, e_sum = sums_all(
+        dp_count, grad_scale, order, norm_gains, sum_a, sum_b, blocks, xf, act, dab, ctx, dproj, wqdf, w1f, w2f
     )
-
-    left_next = stat_decay * left_stat + (1.0 - stat_decay) * jnp.einsum(
-        "sij,skj->sik", own_grad, own_grad, precision=highest
+    outs = finish_all(
+        seq_lengths, row_biases, small, row_accum, as_rows(qkv_bias_accum), as_rows(fc1_bias_accum),
+        own_grad, tokens, out_grad, branch, e_sum, left_stat, right_stat, left_root, right_root,
     )
-    right_next = stat_decay * right_stat + (1.0 - stat_decay) * jnp.einsum(
-        "sji,sjk->sik", own_grad, own_grad, precision=highest
-    )
-    pushed = jnp.einsum("sij,sjk->sik", left_root, own_grad, precision=highest)
-    change = -shampoo_rate * jnp.einsum("sij,sjk->sik", pushed, right_root, precision=highest)
-
-    small = small * grad_scale
-    row_grads = jnp.concatenate([small[:5], small[4:5]], axis=0)
-    row_next, row_change = adagrad_step(row_grads, row_accum)
-    qkv_next, qkv_change = adagrad_step(small[5, : qkv_bias.shape[0]], qkv_bias_accum)
-    fc1_next, fc1_change = adagrad_step(small[6, : fc1_bias.shape[0]], fc1_bias_accum)
+    block_grad, layer_out, input_grad, left_new, right_new, change = outs[:6]
     return (
-        layer_out, input_grad, own_grad, left_next, right_next, change,
-        row_next, row_change, qkv_next, qkv_change, fc1_next, fc1_change,
+        layer_out, input_grad, block_grad, left_new, right_new, change,
+        *outs[6:8], *(v.reshape(-1) for v in outs[8:]),
     )
 
 

time: 264 us -> 221 us (0.84)
  Pallas kernels: 232 us -> 214 us
  matrix products: 13 us -> 0 us
  other arithmetic: 11.4 us -> 2.19 us
    dot_general x4 -> x0, matrix products: 13 us -> none  [the longest x1 4.57 us: shards(): jnp.einsum('sij,skj->sik', own_grad, own_grad, precision=highest)]
    pallas_call x2, Pallas kernels: 60.4 us -> 50.2 us  [the longest x1 38.3 us: hidden_all(): pl.pallas_call(hidden_kernel, out_shape=[jax.ShapeDtypeStruct((rows, hidd...]
    pallas_call x1, Pallas kernels: 79.5 us -> 71.7 us  [sums_all(): pl.pallas_call(functools.partial(sums_kernel, count, scale), out_shape=[j...]
    add x2 -> x0, other arithmetic: 4.95 us -> none  [the longest x1 4.33 us: shards(): grad_out + scale * (e_sum - jnp.mean(e_sum, axis=-1, keepdims=True) - xha...]
    mul x6 -> x0, other arithmetic: 2.8 us -> none  [the longest x4 1.87 us: adagrad_step(): return (accum_next, -adagrad_rate * grad_vec * lax.rsqrt(accum_next))]
where the time goes in v3:
time: 221 us
  Pallas kernels  214 us (97%)
  local copies, waits for them, and re-layouts  3.7 us (2%)
    pallas_call x1, Pallas kernels, mixed_all(): pl.pallas_call(functools.partial(mixed_kernel, count), out_shape=[out(row...  92.2 us
    pallas_call x1, Pallas kernels, sums_all(): pl.pallas_call(functools.partial(sums_kernel, count, scale), out_shape=[j...  71.7 us
    pallas_call x1, Pallas kernels, hidden_all(): pl.pallas_call(hidden_kernel, out_shape=[jax.ShapeDtypeStruct((rows, hidd...  38.3 us
    pallas_call x1, Pallas kernels, finish_all(): pl.pallas_call(functools.partial(finish_kernel, steps), out_shape=[shape(...  11.9 us

profile of v3, /device:TPU:0, one launch (start us, length us, event | category | flops | bytes accessed | tf_op | source)
XLA Modules:
  0.0 220.9 jit_solution(7565517456938293465)
XLA Ops:
  0.6 1.0 fusion.1
  1.6 0.9 copy.34
  2.6 0.7 pad_maximum_fusion.wqd
  3.3 1.8 copy.35
  5.1 92.2 %mixed_all.1 = (bf16[2048,1024]{1,0:T(8,128)(2,1)}, bf16[2048,1024]{1,0:T(8,128)(2,1)}, bf16[2048,1024]{1,0:T(8,128)(2,1)}, bf16[2048,256]{1,0:T(8,128)(2,1)}, b...) custom-call(s32[2]{0:T(128)} %lim_ref.3, ...), custom_call_target="tpu_custom_call" | custom-call | flops 20000000000 | bytes 40000000 | tf_op jit(solution)/shard_map/mixed_all/pallas_call | solution.py:548
  97.3 38.3 %hidden_all.1 = (bf16[2048,1024]{1,0:T(8,128)(2,1)}, bf16[2048,1024]{1,0:T(8,128)(2,1)}, bf16[192,128,128]{2,1,0:T(8,128)(2,1)}, f32[8,1024]{1,0:T(8,128)}) custom-call(f32[2,1024]{1,0:T(2,128)} %gain_ref.5, f32[4,1024]{1,0:T(4,128)} %bias_ref.5, f32[8,128]{1,0:T(8,128)} %bitcast.15, bf16[2048,1024]{1,0:T(8,128)(2,1)} %get-tuple-element.42.x, ...), custom_call_target="tpu_custom_call" | custom-call | flops 22000001024 | bytes 40000000 | tf_op jit(solution)/shard_map/hidden_all/pallas_call | solution.py:672
  135.6 0.8 fusion
  136.4 0.7 select_reduce_fusion.order
  137.1 71.7 %sums_all.1 = (f32[24,128,128]{2,1,0:T(8,128)}, f32[8,1024]{1,0:T(8,128)}, f32[512,1024]{1,0:T(8,128)}, f32[512,1024]{1,0:T(8,128)}) custom-call(s32[192]{0:T(256)} %select_reduce_fusion.order, f32[2,1024]{1,0:T(2,128)} %gain_ref.5, f32[8,1024]{1,0:T(8,128)} %get-tuple-element.41.small_a, f32[8,1024]{1,0:T(8,128)} %get-tuple-element.49.small_b, ...), custom_call_target="tpu_custom_call" | custom-call | flops 12999999488 | bytes 40000000 | tf_op jit(solution)/shard_map/sums_all/pallas_call | solution.py:975
  208.8 11.9 %finish_all.1 = (f32[24,128,128]{2,1,0:T(8,128)}, bf16[512,1024]{1,0:T(8,128)(2,1)}, f32[512,1024]{1,0:T(8,128)}, f32[24,128,128]{2,1,0:T(8,128)}, f32[24,128,12...) custom-call(s32[2]{0:T(128)} %lim_ref.3, ...), custom_call_target="tpu_custom_call" | custom-call | flops 400000000 | bytes 20000000 | tf_op jit(solution)/shard_map/finish_all/pallas_call | solution.py:1079
  (1 shorter events, 0.0 us)
